TPU v7x, 32 devices: a whole 2x2x4 slice. The times are simulated.
32 devices in a mesh: seq: 16 (over z, y, x), dp: 2 (over core).
Axes of the slice: x: 2, y: 2, z: 4, core: 2. Of those that a mesh axis runs over, the one named last changes fastest.
Arguments:
- query_proj: bfloat16 [10240, 1024], P(('dp', 'seq')), parts along dimension 0, may hold values from -8 to 8
- key_proj: bfloat16 [10240, 1024], P(('dp', 'seq')), parts along dimension 0, may hold values from -8 to 8
- value_proj: bfloat16 [10240, 1024], P(('dp', 'seq')), parts along dimension 0, may hold values from -6 to 6
- residual_in: bfloat16 [10240, 1024], P(('dp', 'seq')), parts along dimension 0, may hold values from -6 to 6
- utter_lengths: int32 [32], P('dp'), parts along dimension 0, may hold values from 1 to 640, 5120 in all
- depth_kernel: float32 [31, 1024], replicated, may hold values from -1 to 1
- norm_gain: float32 [1024], replicated, may hold values from 0.5 to 1.5
- norm_shift: float32 [1024], replicated, may hold values from -3 to 3
Outputs:
- block_out: bfloat16 [10240, 1024], P(('dp', 'seq')), parts along dimension 0
There are 2 independent parts, one for each index of `dp`. A program takes and returns all parts, laid end to end along the dimension named above; an argument that names none is the same for every part. Nothing has to cross between parts.
Inputs may be any that keep to these rules, and one draw needn't show every extreme that they name: `utter_lengths`: the lengths sum to 5120; the largest is exactly 640.
All inputs are finite; a program needn't handle non-finite values.
Results may differ from a plain program's by a relative error of at most 0.005.
Values may be sent and summed in bfloat16 or wider, within the bound.
No kernel may reach another device: no remote copies, remote signals or barrier semaphores. Data moves between devices by JAX's collectives and lax.ppermute only.
A program may use at most 64 MiB of HBM per device.

v0:
```python
import functools

import jax
import jax.numpy as jnp
from jax import lax
from jax.experimental import pallas as pl
from jax.experimental.pallas import tpu as pltpu
from jax.sharding import PartitionSpec as P

HD = 64
LANES = 128
GROUP = 4
EDGE = 16
SAME = 2048.0
TAILED = (1, GROUP - 1)
WITH_Q = (2, 3)
KV_BLOCKS = GROUP + 2
WIDTHS = (256, 512, 768, 1024)
SPLIT_VMEM = 56 << 20
ATTEND_VMEM = 24 << 20
FINISH_VMEM = 24 << 20

ANY = pl.BlockSpec(memory_space=pl.ANY)
VMEM = pl.BlockSpec(memory_space=pltpu.VMEM)
SMEM = pl.BlockSpec(memory_space=pltpu.SMEM)


def utterance_of(positions, ends):
    return jnp.sum((ends[None, :] <= positions[:, None]).astype(jnp.int32), axis=1)


def tail_rows(m):
    return 2 * EDGE if m in TAILED else 0


def split_kernel(cols, which, query, key, value, residual, *refs):
    kv_outs, q_outs = refs[:GROUP], refs[GROUP : 2 * GROUP - len(WITH_Q)]
    q_buf, kv_buf, edges, tail, in_sem, out_sem = refs[2 * GROUP - len(WITH_Q) :]
    rows = q_buf.shape[0]
    half = rows // 2
    loads = []
    for i, (src, dst) in enumerate(((key, kv_buf.at[0]), (value, kv_buf.at[1]), (query, q_buf))):
        for part in range(2):
            at = pl.ds(part * half, half)
            sem = in_sem.at[2 * i + part]
            loads.append(pltpu.make_async_copy(src.at[at, :], dst.at[at, :], sem))
    for load in loads:
        load.start()
    tails = [None] * GROUP
    for m in TAILED:
        if m == 1:
            up = which[m] > which[0]
        else:
            up = (which[0] == 1) | (which[0] == GROUP - 1)
        at = pl.multiple_of(jnp.where(up, rows - EDGE, 0), EDGE)
        src = residual.at[pl.ds(at, EDGE), :]
        tails[m] = pltpu.make_async_copy(src, tail.at[m], in_sem.at[6 + m])
        tails[m].start()
    stores = []

    def store(src, dst):
        copy = pltpu.make_async_copy(src, dst, out_sem.at[len(stores)])
        copy.start()
        stores.append(copy)

    mine = [pl.ds(pl.multiple_of(which[m] * cols, LANES), cols) for m in range(GROUP)]
    for i in range(2):
        loads[2 * i].wait()
        loads[2 * i + 1].wait()
        for m in range(GROUP):
            store(kv_buf.at[i, :, mine[m]], kv_outs[m].at[pl.ds(0, rows), pl.ds(i * cols, cols)])
    loads[4].wait()
    loads[5].wait()
    q_alone = [m for m in range(GROUP) if m not in WITH_Q]
    for m in range(GROUP):
        edges[m, :, :cols] = q_buf[:EDGE, mine[m]]
        edges[m, :, cols:] = q_buf[rows - EDGE :, mine[m]]
        if m in WITH_Q:
            at = pl.ds(rows + EDGE + tail_rows(m), half)
            for part in range(2):
                src = q_buf.at[pl.ds(part * half, half), mine[m]]
                store(src, kv_outs[m].at[at, pl.ds(part * cols, cols)])
        else:
            store(q_buf.at[:, mine[m]], q_outs[q_alone.index(m)])
    for m in TAILED:
        tails[m].wait()
        for part in range(2):
            at = pl.ds(rows + (1 + part) * EDGE, EDGE)
            store(tail.at[m, :, pl.ds(part * 2 * cols, 2 * cols)], kv_outs[m].at[at, :])
    for m in range(GROUP):
        store(edges.at[m], kv_outs[m].at[pl.ds(rows, EDGE), :])
    for copy in stores:
        copy.wait()


def split_columns(which, query, key, value, residual):
    rows, width = query.shape
    cols = width // GROUP
    kind = query.dtype
    dma = pltpu.SemaphoreType.DMA
    sizes = [
        rows + EDGE + tail_rows(m) + (rows // 2 if m in WITH_Q else 0) for m in range(GROUP)
    ]
    n_alone = GROUP - len(WITH_Q)
    got = pl.pallas_call(
        functools.partial(split_kernel, cols),
        out_shape=[jax.ShapeDtypeStruct((size, 2 * cols), kind) for size in sizes]
        + [jax.ShapeDtypeStruct((rows, cols), kind)] * n_alone,
        in_specs=[SMEM] + [ANY] * 4,
        out_specs=[ANY] * (GROUP + n_alone),
        scratch_shapes=[
            pltpu.VMEM((rows, width), kind),
            pltpu.VMEM((2, rows, width), kind),
            pltpu.VMEM((GROUP, EDGE, 2 * cols), kind),
            pltpu.VMEM((GROUP, EDGE, width), kind),
            dma((6 + GROUP,)),
            dma((4 * GROUP + 2 * len(TAILED) + len(WITH_Q),)),
        ],
        compiler_params=pltpu.CompilerParams(vmem_limit_bytes=SPLIT_VMEM),
        name="split_columns",
    )(which, query, key, value, residual)
    return got[:GROUP], got[GROUP:]


def attend_kernel(rows, q_rows, widths, q_at, meta, place, starts, ends, *refs):
    kv_in, q_in, outs = refs[:KV_BLOCKS], refs[KV_BLOCKS : KV_BLOCKS + 2], refs[KV_BLOCKS + 2 : KV_BLOCKS + 4]
    q_buf, kv_buf, oh_buf, edges, ctx_buf, q_sem, kv_sem, edge_sem, out_sem = refs[KV_BLOCKS + 4 :]
    cols = q_buf.shape[1]
    half = rows // 2
    blocks = ctx_buf.shape[1] // q_rows
    copies = []
    for i, src in enumerate(kv_in):
        at = pl.multiple_of(place[i] * rows, 16)
        src_rows = src.at[pl.ds(0, rows), :]
        copies.append(pltpu.make_async_copy(src_rows, kv_buf.at[pl.ds(at, rows), :], kv_sem.at[i]))
        src_rows = src.at[pl.ds(rows, EDGE), :]
        copies.append(pltpu.make_async_copy(src_rows, edges.at[place[i]], edge_sem.at[i]))
    for i, src in enumerate(q_in):
        at = pl.multiple_of(place[KV_BLOCKS + i] * rows + EDGE, 16)
        if q_at[i] is None:
            dst = q_buf.at[pl.ds(at, rows), :]
            copies.append(pltpu.make_async_copy(src, dst, q_sem.at[2 * i]))
        else:
            for part in range(2):
                part_of = src.at[pl.ds(q_at[i], half), pl.ds(part * cols, cols)]
                dst = q_buf.at[pl.ds(at + part * half, half), :]
                copies.append(pltpu.make_async_copy(part_of, dst, q_sem.at[2 * i + part]))
    for copy in copies:
        copy.start()

    def one_hot(first, n, value):
        frame = first + lax.broadcasted_iota(jnp.int32, (n, starts.shape[1]), 0)
        inside = (frame >= starts[...]) & (frame < ends[...])
        return jnp.where(inside, jnp.float32(value), jnp.float32(0.0)).astype(jnp.bfloat16)

    @pl.loop(0, kv_buf.shape[0] // half)
    def _(i):
        at = pl.multiple_of(i * half, 16)
        oh_buf[pl.ds(at, half), :] = one_hot(meta[0] + at, half, 1.0)

    for copy in copies:
        copy.wait()
    q_buf[:EDGE, :] = edges[1, :, cols:]
    q_buf[EDGE + 2 * rows :, :] = edges[KV_BLOCKS - 2, :, :cols]

    lane = lax.broadcasted_iota(jnp.int32, (1, LANES), 1)
    scale = HD**-0.5
    halves = [
        jnp.where(lane // HD == h, jnp.float32(scale), jnp.float32(0.0)).astype(jnp.bfloat16)
        for h in range(2)
    ]

    def block(m, b, low, first, width):
        at = pl.multiple_of(b * q_rows, 16)
        oh_q = one_hot(meta[1] + first, q_rows, SAME)
        oh_k = oh_buf[pl.ds(low, width), :]
        oh_both = jnp.concatenate([oh_q, oh_q], axis=0)
        for pair in range(cols // LANES):
            at_cols = slice(pair * LANES, (pair + 1) * LANES)
            v_cols = slice(cols + pair * LANES, cols + (pair + 1) * LANES)
            q = q_buf[pl.ds(first, q_rows), at_cols]
            k = jnp.concatenate([kv_buf[pl.ds(low, width), at_cols], oh_k], axis=1)
            v = kv_buf[pl.ds(low, width), v_cols]
            q_both = jnp.concatenate([q * halves[0], q * halves[1]], axis=0)
            q_both = jnp.concatenate([q_both, oh_both], axis=1)
            s = lax.dot_general(
                q_both, k, (((1,), (1,)), ((), ())), preferred_element_type=jnp.float32
            )
            p = jnp.exp(s - jnp.max(s, axis=1, keepdims=True))
            denom = jnp.sum(p, axis=1, keepdims=True)
            o = jnp.dot(p.astype(jnp.bfloat16), v, preferred_element_type=jnp.float32) / denom
            ctx = jnp.where(lane < HD, o[:q_rows], o[q_rows:])
            ctx_buf[m, pl.ds(at, q_rows), at_cols] = ctx.astype(jnp.bfloat16)

    @pl.loop(0, 2 * blocks)
    def _(t):
        m, b = t // blocks, t % blocks
        first = pl.multiple_of(meta[2 + t], 16)
        low = pl.multiple_of(meta[2 + 2 * blocks + t], 16)
        need = meta[2 + 4 * blocks + t]
        below = 0
        for width in widths:

            @pl.when((need > below) & (need <= width))
            def _(width=width):
                block(m, b, low, first, width)

            below = width

    copies = [pltpu.make_async_copy(ctx_buf.at[m], outs[m], out_sem.at[m]) for m in range(2)]
    for copy in copies:
        copy.start()
    for copy in copies:
        copy.wait()


def attend(rows, cols, q_rows, widths, q_at, meta, place, starts, ends, kv_parts, q_parts):
    keys = KV_BLOCKS * rows
    ext = rows + 2 * EDGE
    shape = jax.ShapeDtypeStruct((ext, cols), jnp.bfloat16)
    dma = pltpu.SemaphoreType.DMA
    return pl.pallas_call(
        functools.partial(attend_kernel, rows, q_rows, widths, q_at),
        out_shape=[shape] * 2,
        in_specs=[SMEM, SMEM, VMEM, VMEM] + [ANY] * (KV_BLOCKS + 2),
        out_specs=[ANY] * 2,
        scratch_shapes=[
            pltpu.VMEM((2 * rows + 2 * EDGE, cols), jnp.bfloat16),
            pltpu.VMEM((keys, 2 * cols), jnp.bfloat16),
            pltpu.VMEM((keys, starts.shape[1]), jnp.bfloat16),
            pltpu.VMEM((KV_BLOCKS, EDGE, 2 * cols), jnp.bfloat16),
            pltpu.VMEM((2, ext, cols), jnp.bfloat16),
            dma((4,)),
            dma((KV_BLOCKS,)),
            dma((KV_BLOCKS,)),
            dma((2,)),
        ],
        compiler_params=pltpu.CompilerParams(vmem_limit_bytes=ATTEND_VMEM),
        cost_estimate=pl.CostEstimate(
            flops=32 * ext * cols * keys, bytes_accessed=8 * keys * cols, transcendentals=0
        ),
        name="attend",
    )(meta, place, starts, ends, *kv_parts, *q_parts)


def finish_kernel(block_rows, taps, meta, starts, ends, *refs):
    ctx_in = refs[:GROUP]
    res, res_before, res_after, kernel, gain, shift, out = refs[GROUP : GROUP + 7]
    mixed, window, conv = refs[GROUP + 7 :]
    rows, width = res.shape
    tiles = width // LANES
    per = tiles // GROUP
    half = taps // 2
    n_blocks = rows // block_rows
    for m in range(GROUP):
        for t in range(per):
            cols = slice(t * LANES, (t + 1) * LANES)
            mixed[meta[1 + m] * per + t] = ctx_in[m][:, cols].astype(jnp.float32)
    for t in range(tiles):
        cols = slice(t * LANES, (t + 1) * LANES)
        for first, part in ((0, res_before), (EDGE, res), (EDGE + rows, res_after)):
            at = slice(first, first + part.shape[0])
            total = part[:, cols].astype(jnp.float32) + mixed[t, at, :]
            mixed[t, at, :] = total.astype(jnp.bfloat16).astype(jnp.float32)

    span = block_rows + 2 * EDGE

    @pl.loop(0, n_blocks)
    def _(b):
        top = pl.multiple_of(b * block_rows, 8)
        first_frame = meta[0] + top
        around = first_frame - EDGE + lax.broadcasted_iota(jnp.int32, (span, LANES), 0)
        frame = first_frame + lax.broadcasted_iota(jnp.int32, (block_rows, LANES), 0)

        @pl.loop(meta[1 + GROUP + b], meta[1 + GROUP + n_blocks + b] + 1)
        def _(u):
            low, high = starts[u], ends[u]
            kept = (around >= low) & (around < high)
            mine = (frame >= low) & (frame < high)
            for t in range(tiles):
                window[t] = jnp.where(kept, mixed[t, pl.ds(top, span), :], jnp.float32(0.0))
            for t in range(tiles):
                cols = slice(t * LANES, (t + 1) * LANES)
                total = jnp.zeros((block_rows, LANES), jnp.float32)
                for tap in range(taps):
                    at = tap + EDGE - half
                    total = total + window[t, at : at + block_rows, :] * kernel[tap : tap + 1, cols]
                conv[t] = jnp.where(mine, total, conv[t])

        values = [conv[t] for t in range(tiles)]
        mean = jnp.sum(sum(values), axis=1, keepdims=True) / width
        centred = [x - mean for x in values]
        var = jnp.sum(sum([x * x for x in centred]), axis=1, keepdims=True) / width
        inverse = 1.0 / jnp.sqrt(var + 1e-05)
        for t in range(tiles):
            cols = slice(t * LANES, (t + 1) * LANES)
            normed = centred[t] * inverse * gain[:, cols] + shift[:, cols]
            gated = normed * jax.nn.sigmoid(normed)
            own = mixed[t, pl.ds(pl.multiple_of(top + EDGE, 8), block_rows), :]
            out[pl.ds(pl.multiple_of(top, 16), block_rows), cols] = (own + gated).astype(
                jnp.bfloat16
            )


def finish(block_rows, meta, starts, ends, ctx_parts, res, before, after, kernel, gain, shift):
    rows, width = res.shape
    tiles = width // LANES
    return pl.pallas_call(
        functools.partial(finish_kernel, block_rows, kernel.shape[0]),
        out_shape=jax.ShapeDtypeStruct((rows, width), jnp.bfloat16),
        in_specs=[SMEM, SMEM, SMEM] + [VMEM] * (GROUP + 6),
        out_specs=VMEM,
        scratch_shapes=[
            pltpu.VMEM((tiles, rows + 2 * EDGE, LANES), jnp.float32),
            pltpu.VMEM((tiles, block_rows + 2 * EDGE, LANES), jnp.float32),
            pltpu.VMEM((tiles, block_rows, LANES), jnp.float32),
        ],
        compiler_params=pltpu.CompilerParams(vmem_limit_bytes=FINISH_VMEM),
        name="finish",
    )(meta, starts, ends, *ctx_parts, res, before, after, kernel, gain, shift)


def local(query, key, value, residual, lengths, depth_kernel, gain, shift):
    rows, width = query.shape
    peers = lax.axis_size("seq")
    frames = rows * peers
    me = lax.axis_index("seq")
    member = me % GROUP
    others = jnp.arange(GROUP, dtype=jnp.int32) ^ member
    halo = 2 * rows
    base = (me - member) * rows

    def swap(array, m):
        return lax.ppermute(array, "seq", [(i, i ^ m) for i in range(peers)])

    def move(array, by):
        pairs = [(i, i + by(i)) for i in range(peers)]
        return lax.ppermute(array, "seq", [(i, j) for i, j in pairs if 0 <= j < peers])

    near = lambda i: -GROUP if i % GROUP < GROUP // 2 else GROUP
    far = lambda i: -near(i)

    kv, q_alone = split_columns(others, query, key, value, residual)
    kv_group = [kv[0]] + [swap(kv[m], m) for m in range(1, GROUP)]
    q_near = [swap(q_alone[1], 1), q_alone[0]]
    bare = [part[: rows + EDGE + tail_rows(m)] for m, part in enumerate(kv_group)]
    kv_halo = [move(bare[m], near if m < 2 else far) for m in range(GROUP)]

    ends = jnp.cumsum(lengths).astype(jnp.int32)
    starts = ends - lengths
    n_utts = lengths.shape[0]
    keys = KV_BLOCKS * rows
    q_rows = (rows + 2 * EDGE) // 2
    halves = jnp.arange(2, dtype=jnp.int32)
    most = -(-(q_rows + 2 * halo + 16) // LANES) * LANES
    widths = sorted({min(w, most) for w in WIDTHS + (most,)})
    pad = -n_utts % LANES
    lane_starts = jnp.pad(starts, (0, pad))[None, :]
    lane_ends = jnp.pad(ends, (0, pad))[None, :]
    first_own = jnp.where(halves == 0, 0, q_rows - EDGE)
    last_own = jnp.where(halves == 0, q_rows - EDGE - 1, rows - 1)

    def attend_pair(ms, kv_parts, q_parts, q_at):
        at = others[ms[0]] // 2
        block_at = jnp.stack([others[m] for m in ms])
        key_base = base + (2 * at - 2) * rows
        first_utt = utterance_of((base + block_at[:, None] * rows + first_own).reshape(-1), ends)
        last_utt = utterance_of((base + block_at[:, None] * rows + last_own).reshape(-1), ends)
        low = (jnp.maximum(starts[first_utt] - key_base, 0) // 16) * 16
        need = jnp.minimum(ends[last_utt] - key_base, keys) - low
        taken = functools.reduce(
            lambda later, w: jnp.where(need <= w, w, later), widths[::-1], jnp.full_like(need, most)
        )
        low = jnp.minimum(low, keys - taken)
        first = ((block_at % 2)[:, None] * rows + halves * q_rows).reshape(-1)
        q_base = base + 2 * at * rows - EDGE
        meta = jnp.concatenate([key_base[None], q_base[None], first, low, need]).astype(jnp.int32)
        halo_at = jnp.stack([others[m] for m in (0, 1)] if ms[0] > 1 else [others[m] for m in (2, 3)])
        place = jnp.concatenate(
            [others - 2 * at + 2, halo_at % 2 + 4 * at, block_at % 2]
        ).astype(jnp.int32)
        return attend(
            rows,
            width // GROUP,
            q_rows,
            widths,
            q_at,
            meta,
            place,
            lane_starts,
            lane_ends,
            kv_parts,
            q_parts,
        )

    q_at = tuple(rows + EDGE + tail_rows(m) for m in (3, 2))
    ctx_far = attend_pair((3, 2), kv_group + kv_halo[:2], [kv_group[3], kv_group[2]], q_at)
    ctx_3, ctx_2 = swap(ctx_far[0], 3), swap(ctx_far[1], 2)
    ctx_near = attend_pair((1, 0), kv_group + kv_halo[2:], q_near, (None, None))
    ctx_group = [ctx_near[1], swap(ctx_near[0], 1), ctx_2, ctx_3]

    def tail_of(part):
        return jnp.concatenate([part[rows + EDGE : rows + 2 * EDGE], part[rows + 2 * EDGE : rows + 3 * EDGE]], axis=1)

    near_tail, diagonal, beyond = tail_of(kv_group[1]), tail_of(kv_group[-1]), tail_of(kv_halo[-1])
    other_tail = jnp.where((member == 0) | (member == GROUP - 1), beyond, diagonal)
    odd = member % 2 == 1
    before = jnp.where(odd, near_tail, other_tail)
    after = jnp.where(odd, other_tail, near_tail)

    block_rows = 32
    n_blocks = rows // block_rows
    block_tops = me * rows + jnp.arange(n_blocks, dtype=jnp.int32) * block_rows
    meta_out = jnp.concatenate(
        [
            (me * rows)[None],
            others,
            utterance_of(block_tops, ends),
            utterance_of(block_tops + block_rows - 1, ends),
        ]
    ).astype(jnp.int32)
    return finish(
        block_rows,
        meta_out,
        starts,
        ends,
        ctx_group,
        residual,
        before,
        after,
        depth_kernel,
        gain[None, :],
        shift[None, :],
    )


def solution(mesh):
    return jax.shard_map(
        local,
        mesh=mesh,
        in_specs=(
            P(("dp", "seq"), None),
            P(("dp", "seq"), None),
            P(("dp", "seq"), None),
            P(("dp", "seq"), None),
            P("dp"),
            P(),
            P(),
            P(),
        ),
        out_specs=P(("dp", "seq"), None),
        check_vma=False,
    )
```

profile of v0, /device:TPU:12, one launch (start us, length us, event | category | flops | bytes accessed | tf_op | source)
XLA Modules:
  0.0 73.3 jit_solution(5450807380031308766)
XLA Ops:
  0.5 3.3 %split_columns.1 = (bf16[336,512]{1,0:T(8,128)(2,1)}, bf16[368,512]{1,0:T(8,128)(2,1)}, bf16[496,512]{1,0:T(8,128)(2,1)}, bf16[528,512]{1,0:T(8,128)(2,1)}, bf16...) custom-call(s32[4]{0:T(128)} %iota_xor_fusion.which, bf16[320,1024]{1,0:T(8,128)(2,1)} %query.1, bf16[320,1024]{1,0:T(8,128)(2,1)} %key.1, ...), custom_call_target="tpu_custom_call" | custom-call | tf_op jit(solution)/shard_map/split_columns/pallas_call | solution.py:105
  3.8 1.6 %collective-permute-start = (bf16[368,512]{1,0:T(8,128)(2,1)}, bf16[368,512]{1,0:T(8,128)(2,1)S(1)}, u32[]{:S(2)}, u32[]{:S(2)}) collective-permute-start(bf16[368,512]{1,0:T(8,128)(2,1)} %get-tuple-element.16), channel_id=1, source_target_pairs={{0,2},{2,0},{4,6},{6,4},{8,10},{10,8},{12,14},{14,12},{16,18},{18,... | collective-permute-start | bytes 1130504 | tf_op jit(solution)/shard_map/ppermute | solution.py:334
  5.9 1.5 %collective-permute-start.2 = (bf16[528,512]{1,0:T(8,128)(2,1)}, bf16[528,512]{1,0:T(8,128)(2,1)S(1)}, u32[]{:S(2)}, u32[]{:S(2)}) collective-permute-start(bf16[528,512]{1,0:T(8,128)(2,1)} %get-tuple-element.18), channel_id=1, source_target_pairs={{0,6},{2,4},{4,2},{6,0},{8,14},{10,12},{12,10},{14,8},{16,22},{18,... | collective-permute-start | bytes 1622024 | tf_op jit(solution)/shard_map/ppermute | solution.py:334
  7.4 1.5 %collective-permute-start.5 = (bf16[320,256]{1,0:T(8,128)(2,1)}, bf16[320,256]{1,0:T(8,128)(2,1)S(1)}, u32[]{:S(2)}, u32[]{:S(2)}) collective-permute-start(bf16[320,256]{1,0:T(8,128)(2,1)} %get-tuple-element.19), channel_id=1, source_target_pairs={{0,2},{2,0},{4,6},{6,4},{8,10},{10,8},{12,14},{14,12},{16,18},{18,... | collective-permute-start | bytes 491528 | tf_op jit(solution)/shard_map/ppermute | solution.py:334
  8.9 3.6 %collective-permute-start.7 = (bf16[336,512]{1,0:T(8,128)(2,1)}, bf16[336,512]{1,0:T(8,128)(2,1)S(1)}, u32[]{:S(2)}, u32[]{:S(2)}) collective-permute-start(bf16[336,512]{1,0:T(8,128)(2,1)} %get-tuple-element.15.refs_0_), channel_id=1, source_target_pairs={{4,12},{6,14},{8,0},{10,2},{12,20},{14,22},{16,8},{18,10},{20,28},... | collective-permute-start | bytes 1032200 | tf_op jit(solution)/shard_map/ppermute | solution.py:338
  12.5 0.7 fusion.19
  18.1 0.6 copy-done.7
  19.0 2.6 %broadcast_multiply_fusion = (s32[2]{0:T(128)S(1)}, s32[2]{0:T(128)S(1)}, s32[2]{0:T(128)S(1)}, s32[2]{0:T(128)S(1)}) fusion(s32[1]{0:T(128)} %get-tuple-element.56, s32[1]{0:T(128)} %get-tuple-element.55, s32[1]{0:T(128)} %get-tuple-element.57, s32[1]{0:T(128)} %get-tuple-element.58), kind=kLoop, calls=%fused_computation.84 | loop fusion | flops 52 | bytes 48 | tf_op jit(solution)/shard_map/mul | solution.py:375
  21.6 2.6 %multiply_add_fusion = (s32[2]{0:T(128)S(1)}, s32[2]{0:T(128)S(1)}) fusion(s32[]{:T(128)S(6)} %mul.97, s32[1]{0:T(128)} %get-tuple-element.56, s32[1]{0:T(128)} %get-tuple-element.55, s32[1]{0:T(128)} %get-tuple-element.57, s32[1]{0:T(128)} %get-tuple-element.58), kind=kLoop, calls=%fused_computation.68 | loop fusion | flops 12 | bytes 36 | tf_op jit(solution)/shard_map/add | solution.py:367
  24.9 0.6 gather_fusion.1
  25.6 0.6 gather_fusion.3
  26.2 0.6 gather_fusion
  28.5 3.5 %collective-permute-start.8 = (bf16[368,512]{1,0:T(8,128)(2,1)S(1)}, bf16[368,512]{1,0:T(8,128)(2,1)S(1)}, u32[]{:S(2)}, u32[]{:S(2)}) collective-permute-start(bf16[368,512]{1,0:T(8,128)(2,1)S(1)} %collective-permute-done.refs_1_), channel_id=1, source_target_pairs={{4,12},{6,14},{8,0},{10,2},{12,20},{14,22},{16,8},{18,10},{20,28},... | collective-permute-start | bytes 1130504 | tf_op jit(solution)/shard_map/ppermute | solution.py:338
  32.0 2.5 %collective-permute-start.3 = (bf16[336,512]{1,0:T(8,128)(2,1)S(1)}, bf16[336,512]{1,0:T(8,128)(2,1)S(1)}, u32[]{:S(2)}, u32[]{:S(2)}) collective-permute-start(bf16[336,512]{1,0:T(8,128)(2,1)S(1)} %slice.64), channel_id=1, source_target_pairs={{0,8},{2,10},{8,16},{10,18},{12,4},{14,6},{16,24},{18,26},{20,12},... | collective-permute-start | bytes 1032200 | tf_op jit(solution)/shard_map/ppermute | solution.py:338
  34.6 1.9 %collective-permute-start.4 = (bf16[368,512]{1,0:T(8,128)(2,1)S(1)}, bf16[368,512]{1,0:T(8,128)(2,1)S(1)}, u32[]{:S(2)}, u32[]{:S(2)}) collective-permute-start(bf16[368,512]{1,0:T(8,128)(2,1)S(1)} %slice.65), channel_id=1, source_target_pairs={{0,8},{2,10},{8,16},{10,18},{12,4},{14,6},{16,24},{18,26},{20,12},... | collective-permute-start | bytes 1130504 | tf_op jit(solution)/shard_map/ppermute | solution.py:338
  36.5 2.9 %collective-permute-done.8.refs_5_ = bf16[368,512]{1,0:T(8,128)(2,1)S(1)} collective-permute-done((bf16[368,512]{1,0:T(8,128)(2,1)S(1)}, bf16[368,512]{1,0:T(8,128)(2,1)S(1)}, u32[]{:S(2)}, u32[]{:S(2)}) %collective-permute-start.8) | collective-permute-done | bytes 376864 | tf_op jit(solution)/shard_map/ppermute | solution.py:338
  39.5 7.8 %attend.3 = (bf16[352,256]{1,0:T(8,128)(2,1)S(1)}, bf16[352,256]{1,0:T(8,128)(2,1)S(1)}) custom-call(s32[14]{0:T(128)S(1)} %concatenate.55.meta, s32[8]{0:T(128)S(1)} %pad_add_fusion.4.place, s32[1,128]{1,0:T(1,128)S(1)} %get-tuple-element.68.starts, s32[1,128]{1,0:T(1,128)S(1)} %get-tuple-element.67.ends, bf16[336,512]{1,0:T(8,128)(2,1)S(1)} %copy-done.4, ...), custom_call_target="tpu_custom_call" | custom-call | flops 5536481280 | bytes 3932160 | tf_op jit(solution)/shard_map/attend/pallas_call | solution.py:222
  47.4 2.0 %collective-permute-start.10 = (bf16[352,256]{1,0:T(8,128)(2,1)S(1)}, bf16[352,256]{1,0:T(8,128)(2,1)S(1)}, u32[]{:S(2)}, u32[]{:S(2)}) collective-permute-start(bf16[352,256]{1,0:T(8,128)(2,1)S(1)} %get-tuple-element.24), channel_id=1, source_target_pairs={{0,6},{2,4},{4,2},{6,0},{8,14},{10,12},{12,10},{14,8},{16,22},{18,... | collective-permute-start | bytes 540680 | tf_op jit(solution)/shard_map/ppermute | solution.py:334
  49.4 0.9 %collective-permute-done.4.refs_5_ = bf16[368,512]{1,0:T(8,128)(2,1)S(1)} collective-permute-done((bf16[368,512]{1,0:T(8,128)(2,1)S(1)}, bf16[368,512]{1,0:T(8,128)(2,1)S(1)}, u32[]{:S(2)}, u32[]{:S(2)}) %collective-permute-start.4) | collective-permute-done | bytes 376864 | tf_op jit(solution)/shard_map/ppermute | solution.py:338
  50.3 9.1 %attend.2 = (bf16[352,256]{1,0:T(8,128)(2,1)S(1)}, bf16[352,256]{1,0:T(8,128)(2,1)S(1)}) custom-call(s32[14]{0:T(128)S(1)} %concatenate.53.meta, s32[8]{0:T(128)S(1)} %pad_add_fusion.2.place, s32[1,128]{1,0:T(1,128)S(1)} %get-tuple-element.68.starts, s32[1,128]{1,0:T(1,128)S(1)} %get-tuple-element.67.ends, bf16[336,512]{1,0:T(8,128)(2,1)S(1)} %copy-done.4, ...), custom_call_target="tpu_custom_call" | custom-call | flops 5536481280 | bytes 3932160 | tf_op jit(solution)/shard_map/attend/pallas_call | solution.py:222
  59.3 0.7 collective-permute-start.6
  60.1 4.8 %collective-permute-done.6.refs_1_ = bf16[352,256]{1,0:T(8,128)(2,1)S(1)} collective-permute-done((bf16[352,256]{1,0:T(8,128)(2,1)S(1)}, bf16[352,256]{1,0:T(8,128)(2,1)S(1)}, u32[]{:S(2)}, u32[]{:S(2)}) %collective-permute-start.6) | collective-permute-done | bytes 180256 | tf_op jit(solution)/shard_map/ppermute | solution.py:334
  64.9 0.7 copy-done.3
  65.6 7.7 %finish.1 = bf16[320,1024]{1,0:T(8,128)(2,1)} custom-call(s32[25]{0:T(128)S(1)} %pad_add_fusion.meta, s32[16]{0:T(128)S(1)} %sub.83.starts, s32[16]{0:T(128)S(1)} %reduce.ends, bf16[352,256]{1,0:T(8,128)(2,1)S(1)} %get-tuple-element.21.refs_0_, bf16[352,256]{1,0:T(8,128)(2,1)S(1)} %collective-permute-done.6.refs_1_, ...), custom_call_target="tpu_custom_call" | custom-call | tf_op jit(solution)/shard_map/finish/pallas_call | solution.py:308
  (68 shorter events, 3.8 us)
Async XLA Ops:
  3.8 24.6 %collective-permute-start = (bf16[368,512]{1,0:T(8,128)(2,1)}, bf16[368,512]{1,0:T(8,128)(2,1)S(1)}, u32[]{:S(2)}, u32[]{:S(2)}) collective-permute-start(bf16[368,512]{1,0:T(8,128)(2,1)} %get-tuple-element.16), channel_id=1, source_target_pairs={{0,2},{2,0},{4,6},{6,4},{8,10},{10,8},{12,14},{14,12},{16,18},{18,... | collective-permute-start | bytes 1130504 | tf_op jit(solution)/shard_map/ppermute | solution.py:334
  5.4 26.6 %collective-permute-start.1 = (bf16[496,512]{1,0:T(8,128)(2,1)}, bf16[496,512]{1,0:T(8,128)(2,1)S(1)}, u32[]{:S(2)}, u32[]{:S(2)}) collective-permute-start(bf16[496,512]{1,0:T(8,128)(2,1)} %get-tuple-element.17), channel_id=1, source_target_pairs={{0,4},{2,6},{4,0},{6,2},{8,12},{10,14},{12,8},{14,10},{16,20},{18,... | collective-permute-start | bytes 1523720 | tf_op jit(solution)/shard_map/ppermute | solution.py:334
  5.9 28.7 %collective-permute-start.2 = (bf16[528,512]{1,0:T(8,128)(2,1)}, bf16[528,512]{1,0:T(8,128)(2,1)S(1)}, u32[]{:S(2)}, u32[]{:S(2)}) collective-permute-start(bf16[528,512]{1,0:T(8,128)(2,1)} %get-tuple-element.18), channel_id=1, source_target_pairs={{0,6},{2,4},{4,2},{6,0},{8,14},{10,12},{12,10},{14,8},{16,22},{18,... | collective-permute-start | bytes 1622024 | tf_op jit(solution)/shard_map/ppermute | solution.py:334
  7.4 42.0 %collective-permute-start.5 = (bf16[320,256]{1,0:T(8,128)(2,1)}, bf16[320,256]{1,0:T(8,128)(2,1)S(1)}, u32[]{:S(2)}, u32[]{:S(2)}) collective-permute-start(bf16[320,256]{1,0:T(8,128)(2,1)} %get-tuple-element.19), channel_id=1, source_target_pairs={{0,2},{2,0},{4,6},{6,4},{8,10},{10,8},{12,14},{14,12},{16,18},{18,... | collective-permute-start | bytes 491528 | tf_op jit(solution)/shard_map/ppermute | solution.py:334
  8.9 3.6 %copy-start.6 = (s32[4]{0:T(128)S(1)}, s32[4]{0:T(128)}, u32[]{:S(2)}) copy-start(s32[4]{0:T(128)} %iota_xor_fusion.which) | copy-start | bytes 52
  8.9 27.7 %collective-permute-start.7 = (bf16[336,512]{1,0:T(8,128)(2,1)}, bf16[336,512]{1,0:T(8,128)(2,1)S(1)}, u32[]{:S(2)}, u32[]{:S(2)}) collective-permute-start(bf16[336,512]{1,0:T(8,128)(2,1)} %get-tuple-element.15.refs_0_), channel_id=1, source_target_pairs={{4,12},{6,14},{8,0},{10,2},{12,20},{14,22},{16,8},{18,10},{20,28},... | collective-permute-start | bytes 1032200 | tf_op jit(solution)/shard_map/ppermute | solution.py:338
  18.0 0.7 copy-start.7
  28.5 11.0 %collective-permute-start.8 = (bf16[368,512]{1,0:T(8,128)(2,1)S(1)}, bf16[368,512]{1,0:T(8,128)(2,1)S(1)}, u32[]{:S(2)}, u32[]{:S(2)}) collective-permute-start(bf16[368,512]{1,0:T(8,128)(2,1)S(1)} %collective-permute-done.refs_1_), channel_id=1, source_target_pairs={{4,12},{6,14},{8,0},{10,2},{12,20},{14,22},{16,8},{18,10},{20,28},... | collective-permute-start | bytes 1130504 | tf_op jit(solution)/shard_map/ppermute | solution.py:338
  32.0 7.5 %copy-start.4 = (bf16[336,512]{1,0:T(8,128)(2,1)S(1)}, bf16[336,512]{1,0:T(8,128)(2,1)}, u32[]{:S(2)}) copy-start(bf16[336,512]{1,0:T(8,128)(2,1)} %get-tuple-element.15.refs_0_) | copy-start | bytes 1032196
  32.0 17.3 %collective-permute-start.3 = (bf16[336,512]{1,0:T(8,128)(2,1)S(1)}, bf16[336,512]{1,0:T(8,128)(2,1)S(1)}, u32[]{:S(2)}, u32[]{:S(2)}) collective-permute-start(bf16[336,512]{1,0:T(8,128)(2,1)S(1)} %slice.64), channel_id=1, source_target_pairs={{0,8},{2,10},{8,16},{10,18},{12,4},{14,6},{16,24},{18,26},{20,12},... | collective-permute-start | bytes 1032200 | tf_op jit(solution)/shard_map/ppermute | solution.py:338
  34.6 15.7 %collective-permute-start.4 = (bf16[368,512]{1,0:T(8,128)(2,1)S(1)}, bf16[368,512]{1,0:T(8,128)(2,1)S(1)}, u32[]{:S(2)}, u32[]{:S(2)}) collective-permute-start(bf16[368,512]{1,0:T(8,128)(2,1)S(1)} %slice.65), channel_id=1, source_target_pairs={{0,8},{2,10},{8,16},{10,18},{12,4},{14,6},{16,24},{18,26},{20,12},... | collective-permute-start | bytes 1130504 | tf_op jit(solution)/shard_map/ppermute | solution.py:338
  39.5 10.8 %copy-start.5 = (bf16[320,256]{1,0:T(8,128)(2,1)S(1)}, bf16[320,256]{1,0:T(8,128)(2,1)}, u32[]{:S(2)}) copy-start(bf16[320,256]{1,0:T(8,128)(2,1)} %get-tuple-element.20.refs_7_) | copy-start | bytes 491524
  47.3 12.8 %collective-permute-start.9 = (bf16[352,256]{1,0:T(8,128)(2,1)S(1)}, bf16[352,256]{1,0:T(8,128)(2,1)S(1)}, u32[]{:S(2)}, u32[]{:S(2)}) collective-permute-start(bf16[352,256]{1,0:T(8,128)(2,1)S(1)} %get-tuple-element.23), channel_id=1, source_target_pairs={{0,4},{2,6},{4,0},{6,2},{8,12},{10,14},{12,8},{14,10},{16,20},{18,... | collective-permute-start | bytes 540680 | tf_op jit(solution)/shard_map/ppermute | solution.py:334
  47.4 12.7 %collective-permute-start.10 = (bf16[352,256]{1,0:T(8,128)(2,1)S(1)}, bf16[352,256]{1,0:T(8,128)(2,1)S(1)}, u32[]{:S(2)}, u32[]{:S(2)}) collective-permute-start(bf16[352,256]{1,0:T(8,128)(2,1)S(1)} %get-tuple-element.24), channel_id=1, source_target_pairs={{0,6},{2,4},{4,2},{6,0},{8,14},{10,12},{12,10},{14,8},{16,22},{18,... | collective-permute-start | bytes 540680 | tf_op jit(solution)/shard_map/ppermute | solution.py:334
  50.3 14.6 %copy-start = (bf16[320,1024]{1,0:T(8,128)(2,1)S(1)}, bf16[320,1024]{1,0:T(8,128)(2,1)}, u32[]{:S(2)}) copy-start(bf16[320,1024]{1,0:T(8,128)(2,1)} %refs_4_.1) | copy-start | bytes 1966084
  59.3 5.6 %copy-start.1 = (f32[31,1024]{1,0:T(8,128)S(1)}, f32[31,1024]{1,0:T(8,128)}, u32[]{:S(2)}) copy-start(f32[31,1024]{1,0:T(8,128)} %refs_7_.1) | copy-start | bytes 380932
  59.3 5.6 %collective-permute-start.6 = (bf16[352,256]{1,0:T(8,128)(2,1)S(1)}, bf16[352,256]{1,0:T(8,128)(2,1)S(1)}, u32[]{:S(2)}, u32[]{:S(2)}) collective-permute-start(bf16[352,256]{1,0:T(8,128)(2,1)S(1)} %get-tuple-element.22), channel_id=1, source_target_pairs={{0,2},{2,0},{4,6},{6,4},{8,10},{10,8},{12,14},{14,12},{16,18},{18,... | collective-permute-start | bytes 540680 | tf_op jit(solution)/shard_map/ppermute | solution.py:334
  64.9 0.7 copy-start.3
  64.9 0.7 copy-start.2
where the time goes:
time: 73.8 us; the launch traced here: 73.3 us
  Pallas kernels  27.9 us (38%)
  starting transfers between devices  19.3 us (26%)
  waiting for transfers between devices  8.69 us (12%)
  other arithmetic  6.96 us (9%)
  local copies, waits for them, and re-layouts  5.38 us (7%)
  between operations  5.13 us (7%)
    pallas_call x2, Pallas kernels, attend(): pl.pallas_call(functools.partial(attend_kernel, rows, q_rows, widths, q_a...  16.8 us
    ppermute x4, starting transfers between devices, move(): lax.ppermute(array, 'seq', [(i, j) for i, j in pairs if 0 <= j < peers])  11.5 us
    ppermute x7, starting transfers between devices, swap(): return lax.ppermute(array, 'seq', [(i, i ^ m) for i in range(peers)])  7.79 us
    pallas_call x1, Pallas kernels, finish(): pl.pallas_call(functools.partial(finish_kernel, block_rows, kernel.shape[...  7.71 us
    ppermute x7, waiting for transfers between devices, swap(): return lax.ppermute(array, 'seq', [(i, i ^ m) for i in range(peers)])  4.85 us
    ppermute x4, waiting for transfers between devices, move(): lax.ppermute(array, 'seq', [(i, j) for i, j in pairs if 0 <= j < peers])  3.84 us
    pallas_call x1, Pallas kernels, split_columns(): pl.pallas_call(functools.partial(split_kernel, cols), out_shape=[jax.Shap...  3.3 us
    add x2, other arithmetic, attend_pair(): base + block_at[:, None] * rows + first_own  2.72 us
  transfers between devices with their start and end apart: 11, of which 3 were waited for; matrix products, arithmetic and copies ran while one was open for 14% of the time, Pallas kernels for 23%

commit v1 on v0

v1 whole, which is shorter than its diff:
```python
import functools

import jax
import jax.numpy as jnp
from jax import lax
from jax.experimental import pallas as pl
from jax.experimental.pallas import tpu as pltpu
from jax.sharding import PartitionSpec as P

HD = 64
LANES = 128
GROUP = 4
EDGE = 16
SAME = 2048.0
TAILED = (1, GROUP - 1)
WITH_Q = (2, 3)
KV_BLOCKS = GROUP + 2
WIDTHS = (256, 512, 768, 1024)
BLOCK_ROWS = 32
SPLIT_VMEM = 56 << 20
ATTEND_VMEM = 24 << 20
FINISH_VMEM = 24 << 20

ANY = pl.BlockSpec(memory_space=pl.ANY)
VMEM = pl.BlockSpec(memory_space=pltpu.VMEM)
SMEM = pl.BlockSpec(memory_space=pltpu.SMEM)


def group_place(rows):
    me = lax.axis_index("seq")
    member = me % GROUP
    return member, (me - member) * rows, [lax.bitwise_xor(member, m) for m in range(GROUP)]


def tail_rows(m):
    return 2 * EDGE if m in TAILED else 0


def split_kernel(cols, query, key, value, residual, *refs):
    kv_outs, q_outs = refs[:GROUP], refs[GROUP : 2 * GROUP - len(WITH_Q)]
    q_buf, kv_buf, edges, tail, in_sem, out_sem = refs[2 * GROUP - len(WITH_Q) :]
    rows = q_buf.shape[0]
    half = rows // 2
    _, _, which = group_place(rows)
    loads = []
    for i, (src, dst) in enumerate(((key, kv_buf.at[0]), (value, kv_buf.at[1]), (query, q_buf))):
        for part in range(2):
            at = pl.ds(part * half, half)
            sem = in_sem.at[2 * i + part]
            loads.append(pltpu.make_async_copy(src.at[at, :], dst.at[at, :], sem))
    for load in loads:
        load.start()
    tails = [None] * GROUP
    for m in TAILED:
        if m == 1:
            up = which[m] > which[0]
        else:
            up = (which[0] == 1) | (which[0] == GROUP - 1)
        at = pl.multiple_of(jnp.where(up, rows - EDGE, 0), EDGE)
        src = residual.at[pl.ds(at, EDGE), :]
        tails[m] = pltpu.make_async_copy(src, tail.at[m], in_sem.at[6 + m])
        tails[m].start()
    stores = []

    def store(src, dst):
        copy = pltpu.make_async_copy(src, dst, out_sem.at[len(stores)])
        copy.start()
        stores.append(copy)

    mine = [pl.ds(pl.multiple_of(which[m] * cols, LANES), cols) for m in range(GROUP)]
    for i in range(2):
        loads[2 * i].wait()
        loads[2 * i + 1].wait()
        for m in range(GROUP):
            store(kv_buf.at[i, :, mine[m]], kv_outs[m].at[pl.ds(0, rows), pl.ds(i * cols, cols)])
    loads[4].wait()
    loads[5].wait()
    q_alone = [m for m in range(GROUP) if m not in WITH_Q]
    for m in range(GROUP):
        edges[m, :, :cols] = q_buf[:EDGE, mine[m]]
        edges[m, :, cols:] = q_buf[rows - EDGE :, mine[m]]
        if m in WITH_Q:
            at = pl.ds(rows + EDGE + tail_rows(m), half)
            for part in range(2):
                src = q_buf.at[pl.ds(part * half, half), mine[m]]
                store(src, kv_outs[m].at[at, pl.ds(part * cols, cols)])
        else:
            store(q_buf.at[:, mine[m]], q_outs[q_alone.index(m)])
    for m in TAILED:
        tails[m].wait()
        for part in range(2):
            at = pl.ds(rows + (1 + part) * EDGE, EDGE)
            store(tail.at[m, :, pl.ds(part * 2 * cols, 2 * cols)], kv_outs[m].at[at, :])
    for m in range(GROUP):
        store(edges.at[m], kv_outs[m].at[pl.ds(rows, EDGE), :])
    for copy in stores:
        copy.wait()


def split_columns(query, key, value, residual):
    rows, width = query.shape
    cols = width // GROUP
    kind = query.dtype
    dma = pltpu.SemaphoreType.DMA
    sizes = [
        rows + EDGE + tail_rows(m) + (rows // 2 if m in WITH_Q else 0) for m in range(GROUP)
    ]
    n_alone = GROUP - len(WITH_Q)
    got = pl.pallas_call(
        functools.partial(split_kernel, cols),
        out_shape=[jax.ShapeDtypeStruct((size, 2 * cols), kind) for size in sizes]
        + [jax.ShapeDtypeStruct((rows, cols), kind)] * n_alone,
        in_specs=[ANY] * 4,
        out_specs=[ANY] * (GROUP + n_alone),
        scratch_shapes=[
            pltpu.VMEM((rows, width), kind),
            pltpu.VMEM((2, rows, width), kind),
            pltpu.VMEM((GROUP, EDGE, 2 * cols), kind),
            pltpu.VMEM((GROUP, EDGE, width), kind),
            dma((6 + GROUP,)),
            dma((4 * GROUP + 2 * len(TAILED) + len(WITH_Q),)),
        ],
        compiler_params=pltpu.CompilerParams(vmem_limit_bytes=SPLIT_VMEM),
        name="split_columns",
    )(query, key, value, residual)
    return got[:GROUP], got[GROUP:]


def attend_kernel(rows, q_rows, widths, ms, q_at, lengths, *refs):
    kv_in, q_in, outs = refs[:KV_BLOCKS], refs[KV_BLOCKS : KV_BLOCKS + 2], refs[KV_BLOCKS + 2 : KV_BLOCKS + 4]
    q_buf, kv_buf, oh_buf, edges, ctx_buf, q_sem, kv_sem, edge_sem, out_sem, meta = refs[
        KV_BLOCKS + 4 :
    ]
    cols = q_buf.shape[1]
    half = rows // 2
    blocks = ctx_buf.shape[1] // q_rows
    _, base, which = group_place(rows)
    pair = which[ms[0]] // 2
    key_base = base + (2 * pair - 2) * rows
    place = [w - 2 * pair + 2 for w in which]
    place += [which[m] % 2 + 4 * pair for m in range(GROUP) if m not in ms]
    place += [which[m] % 2 for m in ms]
    copies = []
    for i, src in enumerate(kv_in):
        at = pl.multiple_of(place[i] * rows, 16)
        src_rows = src.at[pl.ds(0, rows), :]
        copies.append(pltpu.make_async_copy(src_rows, kv_buf.at[pl.ds(at, rows), :], kv_sem.at[i]))
        src_rows = src.at[pl.ds(rows, EDGE), :]
        copies.append(pltpu.make_async_copy(src_rows, edges.at[place[i]], edge_sem.at[i]))
    for i, src in enumerate(q_in):
        at = pl.multiple_of(place[KV_BLOCKS + i] * rows + EDGE, 16)
        if q_at[i] is None:
            dst = q_buf.at[pl.ds(at, rows), :]
            copies.append(pltpu.make_async_copy(src, dst, q_sem.at[2 * i]))
        else:
            for part in range(2):
                part_of = src.at[pl.ds(q_at[i], half), pl.ds(part * cols, cols)]
                dst = q_buf.at[pl.ds(at + part * half, half), :]
                copies.append(pltpu.make_async_copy(part_of, dst, q_sem.at[2 * i + part]))
    for copy in copies:
        copy.start()

    utt_lane = lax.broadcasted_iota(jnp.int32, (1, oh_buf.shape[1]), 1)
    spans = []
    for m in ms:
        own = base + which[m] * rows
        spans += [(own, own + q_rows - EDGE - 1), (own + q_rows - EDGE, own + rows - 1)]

    def visit(u, carry):
        end, low_of, high_of, starts, ends = carry
        start, end = end, end + lengths[u]
        low_of = [jnp.where((a >= start) & (a < end), start, x) for (a, _), x in zip(spans, low_of)]
        high_of = [jnp.where((b >= start) & (b < end), end, x) for (_, b), x in zip(spans, high_of)]
        here = utt_lane == u
        return end, low_of, high_of, jnp.where(here, start, starts), jnp.where(here, end, ends)

    zero, none = jnp.int32(0), jnp.zeros(utt_lane.shape, jnp.int32)
    _, low_of, high_of, starts, ends = lax.fori_loop(
        0, lengths.shape[0], visit, (zero, [zero] * len(spans), [zero] * len(spans), none, none)
    )
    keys = kv_buf.shape[0]
    for t in range(len(spans)):
        low = jnp.maximum(low_of[t] - key_base, 0) // 16 * 16
        need = jnp.minimum(high_of[t] - key_base, keys) - low
        taken = widths[-1]
        for width in widths[-2::-1]:
            taken = jnp.where(need <= width, width, taken)
        meta[0, t] = jnp.minimum(low, keys - taken)
        meta[1, t] = need
        meta[2, t] = which[ms[t // blocks]] % 2 * rows + t % blocks * q_rows

    def one_hot(first, n, value):
        frame = first + lax.broadcasted_iota(jnp.int32, (n, utt_lane.shape[1]), 0)
        inside = (frame >= starts) & (frame < ends)
        return jnp.where(inside, jnp.float32(value), jnp.float32(0.0)).astype(jnp.bfloat16)

    @pl.loop(0, kv_buf.shape[0] // half)
    def _(i):
        at = pl.multiple_of(i * half, 16)
        oh_buf[pl.ds(at, half), :] = one_hot(key_base + at, half, 1.0)

    for copy in copies:
        copy.wait()
    q_buf[:EDGE, :] = edges[1, :, cols:]
    q_buf[EDGE + 2 * rows :, :] = edges[KV_BLOCKS - 2, :, :cols]

    lane = lax.broadcasted_iota(jnp.int32, (1, LANES), 1)
    scale = HD**-0.5
    halves = [
        jnp.where(lane // HD == h, jnp.float32(scale), jnp.float32(0.0)).astype(jnp.bfloat16)
        for h in range(2)
    ]

    def block(m, b, low, first, width):
        at = pl.multiple_of(b * q_rows, 16)
        oh_q = one_hot(key_base + 2 * rows - EDGE + first, q_rows, SAME)
        oh_k = oh_buf[pl.ds(low, width), :]
        oh_both = jnp.concatenate([oh_q, oh_q], axis=0)
        for p_at in range(0, cols, LANES):
            at_cols = slice(p_at, p_at + LANES)
            v_cols = slice(cols + p_at, cols + p_at + LANES)
            q = q_buf[pl.ds(first, q_rows), at_cols]
            k = jnp.concatenate([kv_buf[pl.ds(low, width), at_cols], oh_k], axis=1)
            v = kv_buf[pl.ds(low, width), v_cols]
            q_both = jnp.concatenate([q * halves[0], q * halves[1]], axis=0)
            q_both = jnp.concatenate([q_both, oh_both], axis=1)
            s = lax.dot_general(
                q_both, k, (((1,), (1,)), ((), ())), preferred_element_type=jnp.float32
            )
            p = jnp.exp(s - jnp.max(s, axis=1, keepdims=True))
            denom = jnp.sum(p, axis=1, keepdims=True)
            o = jnp.dot(p.astype(jnp.bfloat16), v, preferred_element_type=jnp.float32) / denom
            ctx = jnp.where(lane < HD, o[:q_rows], o[q_rows:])
            ctx_buf[m, pl.ds(at, q_rows), at_cols] = ctx.astype(jnp.bfloat16)

    @pl.loop(0, 2 * blocks)
    def _(t):
        m, b = t // blocks, t % blocks
        low, need = pl.multiple_of(meta[0, t], 16), meta[1, t]
        first = pl.multiple_of(meta[2, t], 16)
        below = 0
        for width in widths:

            @pl.when((need > below) & (need <= width))
            def _(width=width):
                block(m, b, low, first, width)

            below = width

    copies = [pltpu.make_async_copy(ctx_buf.at[m], outs[m], out_sem.at[m]) for m in range(2)]
    for copy in copies:
        copy.start()
    for copy in copies:
        copy.wait()


def attend(rows, cols, ms, q_at, lengths, kv_parts, q_parts):
    keys = KV_BLOCKS * rows
    ext = rows + 2 * EDGE
    q_rows = ext // 2
    most = -(-(q_rows + 4 * rows + 16) // LANES) * LANES
    widths = sorted({min(w, most) for w in WIDTHS + (most,)})
    utts = -(-lengths.shape[0] // LANES) * LANES
    shape = jax.ShapeDtypeStruct((ext, cols), jnp.bfloat16)
    dma = pltpu.SemaphoreType.DMA
    return pl.pallas_call(
        functools.partial(attend_kernel, rows, q_rows, widths, ms, q_at),
        out_shape=[shape] * 2,
        in_specs=[SMEM] + [ANY] * (KV_BLOCKS + 2),
        out_specs=[ANY] * 2,
        scratch_shapes=[
            pltpu.VMEM((2 * rows + 2 * EDGE, cols), jnp.bfloat16),
            pltpu.VMEM((keys, 2 * cols), jnp.bfloat16),
            pltpu.VMEM((keys, utts), jnp.bfloat16),
            pltpu.VMEM((KV_BLOCKS, EDGE, 2 * cols), jnp.bfloat16),
            pltpu.VMEM((2, ext, cols), jnp.bfloat16),
            dma((4,)),
            dma((KV_BLOCKS,)),
            dma((KV_BLOCKS,)),
            dma((2,)),
            pltpu.SMEM((3, 4), jnp.int32),
        ],
        compiler_params=pltpu.CompilerParams(vmem_limit_bytes=ATTEND_VMEM),
        cost_estimate=pl.CostEstimate(
            flops=32 * ext * cols * keys, bytes_accessed=8 * keys * cols, transcendentals=0
        ),
        name="attend",
    )(lengths, *kv_parts, *q_parts)


def convolve(block_rows, ms, lengths, ctx_in, res, before, after, kernel, mixed_out, conv_out, scratch):
    mixed, window, starts, ends = scratch
    rows, width = res.shape
    _, base, which = group_place(rows)
    own = base + which[0] * rows
    per = width // LANES // GROUP
    taps = kernel.shape[0]
    half = taps // 2
    tiles = [
        (i, t, pl.ds(pl.multiple_of((which[m] * per + t) * LANES, LANES), LANES))
        for i, m in enumerate(ms)
        for t in range(per)
    ]

    def note(u, end):
        starts[u] = end
        ends[u] = end + lengths[u]
        return end + lengths[u]

    lax.fori_loop(0, lengths.shape[0], note, jnp.int32(0))
    for slot, (i, t, cols) in enumerate(tiles):
        ctx = ctx_in[i][:, t * LANES : (t + 1) * LANES].astype(jnp.float32)
        for first, part in ((0, before), (EDGE, res), (EDGE + rows, after)):
            at = slice(first, first + part.shape[0])
            total = (part[:, cols].astype(jnp.float32) + ctx[at]).astype(jnp.bfloat16)
            mixed[slot, at, :] = total.astype(jnp.float32)
            if part is res:
                mixed_out[slot] = total

    span = block_rows + 2 * EDGE

    def past(frame):
        return lambda u: ends[u] <= frame

    @pl.loop(0, rows // block_rows, init_carry=jnp.int32(0))
    def _(b, first_utt):
        top = pl.multiple_of(b * block_rows, 16)
        around = own + top - EDGE + lax.broadcasted_iota(jnp.int32, (span, LANES), 0)
        frame = own + top + lax.broadcasted_iota(jnp.int32, (block_rows, LANES), 0)
        first_utt = lax.while_loop(past(own + top), lambda u: u + 1, first_utt)
        last_utt = lax.while_loop(past(own + top + block_rows - 1), lambda u: u + 1, first_utt)

        @pl.loop(first_utt, last_utt + 1)
        def _(u):
            low, high = starts[u], ends[u]
            kept = (around >= low) & (around < high)
            mine = (frame >= low) & (frame < high)
            for slot in range(len(tiles)):
                window[slot] = jnp.where(kept, mixed[slot, pl.ds(top, span), :], jnp.float32(0.0))
            for slot, (_, _, cols) in enumerate(tiles):
                total = jnp.zeros((block_rows, LANES), jnp.float32)
                for tap in range(taps):
                    at = tap + EDGE - half
                    total = total + window[slot, at : at + block_rows, :] * kernel[tap : tap + 1, cols]
                at = pl.ds(top, block_rows)
                conv_out[slot, at, :] = jnp.where(mine, total, conv_out[slot, at, :])

        return last_utt


def convolve_kernel(block_rows, ms, lengths, *refs):
    ctx_in = refs[: len(ms)]
    res, before, after, kernel, mixed_out, conv_out = refs[len(ms) : len(ms) + 6]
    scratch = refs[len(ms) + 6 :]
    convolve(block_rows, ms, lengths, ctx_in, res, before, after, kernel, mixed_out, conv_out, scratch)


def finish_kernel(block_rows, ms, early, lengths, *refs):
    ctx_in = refs[: len(ms)]
    res, before, after, kernel, gain, shift, mixed_in, conv_in, out = refs[len(ms) : len(ms) + 9]
    mixed_own, conv_own = refs[len(ms) + 9 : len(ms) + 11]
    scratch = refs[len(ms) + 11 :]
    convolve(block_rows, ms, lengths, ctx_in, res, before, after, kernel, mixed_own, conv_own, scratch)
    rows, width = res.shape
    _, _, which = group_place(rows)
    per = width // LANES // GROUP
    sources = []
    for group, mixed, conv in ((early, mixed_in, conv_in), (ms, mixed_own, conv_own)):
        for i, m in enumerate(group):
            for t in range(per):
                cols = pl.ds(pl.multiple_of((which[m] * per + t) * LANES, LANES), LANES)
                sources.append((mixed, conv, i * per + t, cols))

    @pl.loop(0, rows // block_rows)
    def _(b):
        at = pl.ds(pl.multiple_of(b * block_rows, 16), block_rows)
        values = [conv[slot, at, :] for _, conv, slot, _ in sources]
        mean = jnp.sum(sum(values), axis=1, keepdims=True) / width
        centred = [x - mean for x in values]
        var = jnp.sum(sum([x * x for x in centred]), axis=1, keepdims=True) / width
        inverse = 1.0 / jnp.sqrt(var + 1e-05)
        for x, (mixed, _, slot, cols) in zip(centred, sources):
            normed = x * inverse * gain[:, cols] + shift[:, cols]
            gated = normed * jax.nn.sigmoid(normed)
            out[at, cols] = (mixed[slot, at, :].astype(jnp.float32) + gated).astype(jnp.bfloat16)


def conv_scratch(slots, rows, block_rows, utts):
    return [
        pltpu.VMEM((slots, rows + 2 * EDGE, LANES), jnp.float32),
        pltpu.VMEM((slots, block_rows + 2 * EDGE, LANES), jnp.float32),
        pltpu.SMEM((utts,), jnp.int32),
        pltpu.SMEM((utts,), jnp.int32),
    ]


def convolve_early(ms, lengths, ctx_parts, res, before, after, kernel):
    rows, width = res.shape
    slots = len(ms) * width // LANES // GROUP
    taps = kernel.shape[0]
    return pl.pallas_call(
        functools.partial(convolve_kernel, BLOCK_ROWS, ms),
        out_shape=[
            jax.ShapeDtypeStruct((slots, rows, LANES), jnp.bfloat16),
            jax.ShapeDtypeStruct((slots, rows, LANES), jnp.float32),
        ],
        in_specs=[SMEM] + [VMEM] * (len(ms) + 4),
        out_specs=[VMEM] * 2,
        scratch_shapes=conv_scratch(slots, rows, BLOCK_ROWS, lengths.shape[0]),
        compiler_params=pltpu.CompilerParams(vmem_limit_bytes=FINISH_VMEM),
        cost_estimate=pl.CostEstimate(
            flops=100 * taps * rows * slots * LANES, bytes_accessed=8 * rows * width, transcendentals=0
        ),
        name="convolve",
    )(lengths, *ctx_parts, res, before, after, kernel)


def finish(ms, early, lengths, ctx_parts, res, before, after, kernel, gain, shift, mixed, conv):
    rows, width = res.shape
    slots = len(ms) * width // LANES // GROUP
    return pl.pallas_call(
        functools.partial(finish_kernel, BLOCK_ROWS, ms, early),
        out_shape=jax.ShapeDtypeStruct((rows, width), jnp.bfloat16),
        in_specs=[SMEM] + [VMEM] * (len(ms) + 8),
        out_specs=VMEM,
        scratch_shapes=[
            pltpu.VMEM((slots, rows, LANES), jnp.bfloat16),
            pltpu.VMEM((slots, rows, LANES), jnp.float32),
        ]
        + conv_scratch(slots, rows, BLOCK_ROWS, lengths.shape[0]),
        compiler_params=pltpu.CompilerParams(vmem_limit_bytes=FINISH_VMEM),
        name="finish",
    )(lengths, *ctx_parts, res, before, after, kernel, gain, shift, mixed, conv)


def local(query, key, value, residual, lengths, depth_kernel, gain, shift):
    rows, width = query.shape
    cols = width // GROUP
    peers = lax.axis_size("seq")

    def swap(array, m):
        return lax.ppermute(array, "seq", [(i, i ^ m) for i in range(peers)])

    def move(array, by):
        pairs = [(i, i + by(i)) for i in range(peers)]
        return lax.ppermute(array, "seq", [(i, j) for i, j in pairs if 0 <= j < peers])

    near = lambda i: -GROUP if i % GROUP < GROUP // 2 else GROUP
    far = lambda i: -near(i)

    kv, q_alone = split_columns(query, key, value, residual)
    kv_group = [kv[0]] + [swap(kv[m], m) for m in range(1, GROUP)]
    q_near = [swap(q_alone[1], 1), q_alone[0]]
    bare = [part[: rows + EDGE + tail_rows(m)] for m, part in enumerate(kv_group)]
    kv_halo = [move(bare[m], near if m < 2 else far) for m in range(GROUP)]

    q_at = tuple(rows + EDGE + tail_rows(m) for m in (3, 2))
    far_q = [kv_group[3], kv_group[2]]
    ctx_far = attend(rows, cols, (3, 2), q_at, lengths, kv_group + kv_halo[:2], far_q)
    ctx_3, ctx_2 = swap(ctx_far[0], 3), swap(ctx_far[1], 2)
    ctx_near = attend(rows, cols, (1, 0), (None, None), lengths, kv_group + kv_halo[2:], q_near)
    ctx_1 = swap(ctx_near[0], 1)

    def tail_of(part):
        tail = part[rows + EDGE : rows + 3 * EDGE]
        return jnp.concatenate([tail[:EDGE], tail[EDGE:]], axis=1)

    member = lax.axis_index("seq") % GROUP
    near_tail, diagonal, beyond = tail_of(kv_group[1]), tail_of(kv_group[3]), tail_of(kv_halo[3])
    other_tail = jnp.where((member == 0) | (member == GROUP - 1), beyond, diagonal)
    odd = member % 2 == 1
    before = jnp.where(odd, near_tail, other_tail)
    after = jnp.where(odd, other_tail, near_tail)

    around = (residual, before, after, depth_kernel)
    early = (0, 2, 3)
    mixed, conv = convolve_early(early, lengths, [ctx_near[1], ctx_2, ctx_3], *around)
    late = (1,)
    return finish(late, early, lengths, [ctx_1], *around, gain[None, :], shift[None, :], mixed, conv)


def solution(mesh):
    return jax.shard_map(
        local,
        mesh=mesh,
        in_specs=(
            P(("dp", "seq"), None),
            P(("dp", "seq"), None),
            P(("dp", "seq"), None),
            P(("dp", "seq"), None),
            P("dp"),
            P(),
            P(),
            P(),
        ),
        out_specs=P(("dp", "seq"), None),
        check_vma=False,
    )
```

time: 73.8 us -> 69.5 us (0.942)
  the two profiles are of different devices: /device:TPU:12 before, /device:TPU:0 now
where the time goes in v1:
time: 69.5 us; the launch traced here: 68.6 us
  Pallas kernels  26.7 us (38%)
  starting transfers between devices  20.7 us (30%)
  waiting for transfers between devices  20.6 us (30%)
    ppermute x7, waiting for transfers between devices, swap(): return lax.ppermute(array, 'seq', [(i, i ^ m) for i in range(peers)])  20.4 us
    pallas_call x2, Pallas kernels, attend(): pl.pallas_call(functools.partial(attend_kernel, rows, q_rows, widths, ms,...  15.5 us
    ppermute x7, starting transfers between devices, swap(): return lax.ppermute(array, 'seq', [(i, i ^ m) for i in range(peers)])  11.1 us
    ppermute x4, starting transfers between devices, move(): lax.ppermute(array, 'seq', [(i, j) for i, j in pairs if 0 <= j < peers])  9.68 us
    pallas_call x1, Pallas kernels, finish(): pl.pallas_call(functools.partial(finish_kernel, BLOCK_ROWS, ms, early), o...  5.03 us
    pallas_call x1, Pallas kernels, convolve_early(): pl.pallas_call(functools.partial(convolve_kernel, BLOCK_ROWS, ms), out_sh...  3.45 us
    pallas_call x1, Pallas kernels, split_columns(): pl.pallas_call(functools.partial(split_kernel, cols), out_shape=[jax.Shap...  2.64 us
  transfers between devices with their start and end apart: 11, of which 4 were waited for; matrix products, arithmetic and copies ran while one was open for 0% of the time, Pallas kernels for 28%

profile of v1, /device:TPU:0, one launch (start us, length us, event | category | flops | bytes accessed | tf_op | source)
XLA Modules:
  0.0 68.6 jit_solution(10741180402512588383)
XLA Ops:
  0.0 2.6 %split_columns.1 = (bf16[336,512]{1,0:T(8,128)(2,1)}, bf16[368,512]{1,0:T(8,128)(2,1)}, bf16[496,512]{1,0:T(8,128)(2,1)}, bf16[528,512]{1,0:T(8,128)(2,1)}, bf16...) custom-call(bf16[320,1024]{1,0:T(8,128)(2,1)} %query.1, bf16[320,1024]{1,0:T(8,128)(2,1)} %key.1, bf16[320,1024]{1,0:T(8,128)(2,1)} %value.1, ...), custom_call_target="tpu_custom_call" | custom-call | tf_op jit(solution)/shard_map/split_columns/pallas_call | solution.py:109
  2.6 3.0 %collective-permute-start = (bf16[368,512]{1,0:T(8,128)(2,1)}, bf16[368,512]{1,0:T(8,128)(2,1)S(1)}, u32[]{:S(2)}, u32[]{:S(2)}) collective-permute-start(bf16[368,512]{1,0:T(8,128)(2,1)} %get-tuple-element.18), channel_id=1, source_target_pairs={{0,2},{2,0},{4,6},{6,4},{8,10},{10,8},{12,14},{14,12},{16,18},{18,... | collective-permute-start | bytes 1130504 | tf_op jit(solution)/shard_map/ppermute | solution.py:442
  5.7 1.5 %collective-permute-start.2 = (bf16[528,512]{1,0:T(8,128)(2,1)}, bf16[528,512]{1,0:T(8,128)(2,1)S(1)}, u32[]{:S(2)}, u32[]{:S(2)}) collective-permute-start(bf16[528,512]{1,0:T(8,128)(2,1)} %get-tuple-element.20), channel_id=1, source_target_pairs={{0,6},{2,4},{4,2},{6,0},{8,14},{10,12},{12,10},{14,8},{16,22},{18,... | collective-permute-start | bytes 1622024 | tf_op jit(solution)/shard_map/ppermute | solution.py:442
  7.1 0.0 collective-permute-start.1
  7.2 1.9 %collective-permute-start.5 = (bf16[320,256]{1,0:T(8,128)(2,1)}, bf16[320,256]{1,0:T(8,128)(2,1)S(1)}, u32[]{:S(2)}, u32[]{:S(2)}) collective-permute-start(bf16[320,256]{1,0:T(8,128)(2,1)} %get-tuple-element.21), channel_id=1, source_target_pairs={{0,2},{2,0},{4,6},{6,4},{8,10},{10,8},{12,14},{14,12},{16,18},{18,... | collective-permute-start | bytes 491528 | tf_op jit(solution)/shard_map/ppermute | solution.py:442
  9.1 1.3 %collective-permute-start.7 = (bf16[336,512]{1,0:T(8,128)(2,1)}, bf16[336,512]{1,0:T(8,128)(2,1)S(1)}, u32[]{:S(2)}, u32[]{:S(2)}) collective-permute-start(bf16[336,512]{1,0:T(8,128)(2,1)} %get-tuple-element.17.refs_0_), channel_id=1, source_target_pairs={{4,12},{6,14},{8,0},{10,2},{12,20},{14,22},{16,8},{18,10},{20,28},... | collective-permute-start | bytes 1032200 | tf_op jit(solution)/shard_map/ppermute | solution.py:446
  10.5 5.0 %collective-permute-done.refs_1_ = bf16[368,512]{1,0:T(8,128)(2,1)S(1)} collective-permute-done((bf16[368,512]{1,0:T(8,128)(2,1)}, bf16[368,512]{1,0:T(8,128)(2,1)S(1)}, u32[]{:S(2)}, u32[]{:S(2)}) %collective-permute-start) | collective-permute-done | bytes 376864 | tf_op jit(solution)/shard_map/ppermute | solution.py:442
  15.5 1.3 %collective-permute-start.8 = (bf16[368,512]{1,0:T(8,128)(2,1)S(1)}, bf16[368,512]{1,0:T(8,128)(2,1)S(1)}, u32[]{:S(2)}, u32[]{:S(2)}) collective-permute-start(bf16[368,512]{1,0:T(8,128)(2,1)S(1)} %collective-permute-done.refs_1_), channel_id=1, source_target_pairs={{4,12},{6,14},{8,0},{10,2},{12,20},{14,22},{16,8},{18,10},{20,28},... | collective-permute-start | bytes 1130504 | tf_op jit(solution)/shard_map/ppermute | solution.py:446
  16.8 14.9 %collective-permute-done.1.refs_2_.refs_7_ = bf16[496,512]{1,0:T(8,128)(2,1)S(1)} collective-permute-done((bf16[496,512]{1,0:T(8,128)(2,1)}, bf16[496,512]{1,0:T(8,128)(2,1)S(1)}, u32[]{:S(2)}, u32[]{:S(2)}) %collective-permute-start.1) | collective-permute-done | bytes 507936 | tf_op jit(solution)/shard_map/ppermute | solution.py:442
  31.7 3.6 %collective-permute-start.3 = (bf16[336,512]{1,0:T(8,128)(2,1)S(1)}, bf16[336,512]{1,0:T(8,128)(2,1)S(1)}, u32[]{:S(2)}, u32[]{:S(2)}) collective-permute-start(bf16[336,512]{1,0:T(8,128)(2,1)S(1)} %slice.41), channel_id=1, source_target_pairs={{0,8},{2,10},{8,16},{10,18},{12,4},{14,6},{16,24},{18,26},{20,12},... | collective-permute-start | bytes 1032200 | tf_op jit(solution)/shard_map/ppermute | solution.py:446
  35.4 0.0 copy-start.4
  35.4 3.5 %collective-permute-start.4 = (bf16[368,512]{1,0:T(8,128)(2,1)S(1)}, bf16[368,512]{1,0:T(8,128)(2,1)S(1)}, u32[]{:S(2)}, u32[]{:S(2)}) collective-permute-start(bf16[368,512]{1,0:T(8,128)(2,1)S(1)} %slice.42), channel_id=1, source_target_pairs={{0,8},{2,10},{8,16},{10,18},{12,4},{14,6},{16,24},{18,26},{20,12},... | collective-permute-start | bytes 1130504 | tf_op jit(solution)/shard_map/ppermute | solution.py:446
  39.0 7.1 %attend.3 = (bf16[352,256]{1,0:T(8,128)(2,1)S(1)}, bf16[352,256]{1,0:T(8,128)(2,1)S(1)}) custom-call(s32[16]{0:T(128)S(1)} %copy-done.4, bf16[336,512]{1,0:T(8,128)(2,1)S(1)} %copy-done.5, bf16[368,512]{1,0:T(8,128)(2,1)S(1)} %collective-permute-done.refs_1_, bf16[496,512]{1,0:T(8,128)(2,1)S(1)} %collective-permute-done.1.refs_2_.refs_7_, ...), custom_call_target="tpu_custom_call" | custom-call | flops 5536481280 | bytes 3932160 | tf_op jit(solution)/shard_map/attend/pallas_call | solution.py:266
  46.0 0.1 collective-permute-start.9
  46.1 2.9 %collective-permute-start.10 = (bf16[352,256]{1,0:T(8,128)(2,1)S(1)}, bf16[352,256]{1,0:T(8,128)(2,1)S(1)}, u32[]{:S(2)}, u32[]{:S(2)}) collective-permute-start(bf16[352,256]{1,0:T(8,128)(2,1)S(1)} %get-tuple-element.26), channel_id=1, source_target_pairs={{0,6},{2,4},{4,2},{6,0},{8,14},{10,12},{12,10},{14,8},{16,22},{18,... | collective-permute-start | bytes 540680 | tf_op jit(solution)/shard_map/ppermute | solution.py:442
  49.1 0.2 collective-permute-done.4.refs_5_
  49.2 8.5 %attend.2 = (bf16[352,256]{1,0:T(8,128)(2,1)S(1)}, bf16[352,256]{1,0:T(8,128)(2,1)S(1)}) custom-call(s32[16]{0:T(128)S(1)} %copy-done.4, bf16[336,512]{1,0:T(8,128)(2,1)S(1)} %copy-done.5, bf16[368,512]{1,0:T(8,128)(2,1)S(1)} %collective-permute-done.refs_1_, bf16[496,512]{1,0:T(8,128)(2,1)S(1)} %collective-permute-done.1.refs_2_.refs_7_, ...), custom_call_target="tpu_custom_call" | custom-call | flops 5536481280 | bytes 3932160 | tf_op jit(solution)/shard_map/attend/pallas_call | solution.py:266
  57.7 0.0 copy-start.1
  57.8 1.6 %collective-permute-start.6 = (bf16[352,256]{1,0:T(8,128)(2,1)S(1)}, bf16[352,256]{1,0:T(8,128)(2,1)S(1)}, u32[]{:S(2)}, u32[]{:S(2)}) collective-permute-start(bf16[352,256]{1,0:T(8,128)(2,1)S(1)} %get-tuple-element.23), channel_id=1, source_target_pairs={{0,2},{2,0},{4,6},{6,4},{8,10},{10,8},{12,14},{14,12},{16,18},{18,... | collective-permute-start | bytes 540680 | tf_op jit(solution)/shard_map/ppermute | solution.py:442
  59.4 0.0 copy-start.3
  59.4 3.5 %convolve.1 = (bf16[6,320,128]{2,1,0:T(8,128)(2,1)S(1)}, f32[6,320,128]{2,1,0:T(8,128)S(1)}) custom-call(s32[16]{0:T(128)S(1)} %copy-done.4, bf16[352,256]{1,0:T(8,128)(2,1)S(1)} %get-tuple-element.24.refs_0_, bf16[352,256]{1,0:T(8,128)(2,1)S(1)} %collective-permute-done.9.refs_1_, bf16[352,256]{1,0:T(8,128)(2,1)S(1)} %collective-permute-done.10.refs_2_, ...), custom_call_target="tpu_custom_call" | custom-call | flops 761856000 | bytes 2621440 | tf_op jit(solution)/shard_map/convolve/pallas_call | solution.py:401
  62.9 0.4 collective-permute-done.6.refs_0_
  63.3 0.2 copy-done.2
  63.5 5.0 %finish.1 = bf16[320,1024]{1,0:T(8,128)(2,1)} custom-call(s32[16]{0:T(128)S(1)} %copy-done.4, bf16[352,256]{1,0:T(8,128)(2,1)S(1)} %collective-permute-done.6.refs_0_, bf16[320,1024]{1,0:T(8,128)(2,1)S(1)} %copy-done, bf16[16,1024]{1,0:T(8,128)(2,1)S(1)} %get-tuple-element.36.refs_4_.refs_2_, bf16[16,1024]{1,0:T(8,128)(2,1)S(1)} %get-tuple-element.35.refs_5_.refs_3_, ...), custom_call_target="tpu_custom_call" | custom-call | tf_op jit(solution)/shard_map/finish/pallas_call | solution.py:421
  (23 shorter events, 0.1 us)
Async XLA Ops:
  2.6 12.8 %collective-permute-start = (bf16[368,512]{1,0:T(8,128)(2,1)}, bf16[368,512]{1,0:T(8,128)(2,1)S(1)}, u32[]{:S(2)}, u32[]{:S(2)}) collective-permute-start(bf16[368,512]{1,0:T(8,128)(2,1)} %get-tuple-element.18), channel_id=1, source_target_pairs={{0,2},{2,0},{4,6},{6,4},{8,10},{10,8},{12,14},{14,12},{16,18},{18,... | collective-permute-start | bytes 1130504 | tf_op jit(solution)/shard_map/ppermute | solution.py:442
  5.7 29.7 %collective-permute-start.2 = (bf16[528,512]{1,0:T(8,128)(2,1)}, bf16[528,512]{1,0:T(8,128)(2,1)S(1)}, u32[]{:S(2)}, u32[]{:S(2)}) collective-permute-start(bf16[528,512]{1,0:T(8,128)(2,1)} %get-tuple-element.20), channel_id=1, source_target_pairs={{0,6},{2,4},{4,2},{6,0},{8,14},{10,12},{12,10},{14,8},{16,22},{18,... | collective-permute-start | bytes 1622024 | tf_op jit(solution)/shard_map/ppermute | solution.py:442
  7.1 24.5 %collective-permute-start.1 = (bf16[496,512]{1,0:T(8,128)(2,1)}, bf16[496,512]{1,0:T(8,128)(2,1)S(1)}, u32[]{:S(2)}, u32[]{:S(2)}) collective-permute-start(bf16[496,512]{1,0:T(8,128)(2,1)} %get-tuple-element.19), channel_id=1, source_target_pairs={{0,4},{2,6},{4,0},{6,2},{8,12},{10,14},{12,8},{14,10},{16,20},{18,... | collective-permute-start | bytes 1523720 | tf_op jit(solution)/shard_map/ppermute | solution.py:442
  7.2 41.9 %collective-permute-start.5 = (bf16[320,256]{1,0:T(8,128)(2,1)}, bf16[320,256]{1,0:T(8,128)(2,1)S(1)}, u32[]{:S(2)}, u32[]{:S(2)}) collective-permute-start(bf16[320,256]{1,0:T(8,128)(2,1)} %get-tuple-element.21), channel_id=1, source_target_pairs={{0,2},{2,0},{4,6},{6,4},{8,10},{10,8},{12,14},{14,12},{16,18},{18,... | collective-permute-start | bytes 491528 | tf_op jit(solution)/shard_map/ppermute | solution.py:442
  9.1 29.8 %collective-permute-start.7 = (bf16[336,512]{1,0:T(8,128)(2,1)}, bf16[336,512]{1,0:T(8,128)(2,1)S(1)}, u32[]{:S(2)}, u32[]{:S(2)}) collective-permute-start(bf16[336,512]{1,0:T(8,128)(2,1)} %get-tuple-element.17.refs_0_), channel_id=1, source_target_pairs={{4,12},{6,14},{8,0},{10,2},{12,20},{14,22},{16,8},{18,10},{20,28},... | collective-permute-start | bytes 1032200 | tf_op jit(solution)/shard_map/ppermute | solution.py:446
  15.5 23.5 %collective-permute-start.8 = (bf16[368,512]{1,0:T(8,128)(2,1)S(1)}, bf16[368,512]{1,0:T(8,128)(2,1)S(1)}, u32[]{:S(2)}, u32[]{:S(2)}) collective-permute-start(bf16[368,512]{1,0:T(8,128)(2,1)S(1)} %collective-permute-done.refs_1_), channel_id=1, source_target_pairs={{4,12},{6,14},{8,0},{10,2},{12,20},{14,22},{16,8},{18,10},{20,28},... | collective-permute-start | bytes 1130504 | tf_op jit(solution)/shard_map/ppermute | solution.py:446
  31.7 7.2 %copy-start.5 = (bf16[336,512]{1,0:T(8,128)(2,1)S(1)}, bf16[336,512]{1,0:T(8,128)(2,1)}, u32[]{:S(2)}) copy-start(bf16[336,512]{1,0:T(8,128)(2,1)} %get-tuple-element.17.refs_0_) | copy-start | bytes 1032196
  31.7 17.3 %collective-permute-start.3 = (bf16[336,512]{1,0:T(8,128)(2,1)S(1)}, bf16[336,512]{1,0:T(8,128)(2,1)S(1)}, u32[]{:S(2)}, u32[]{:S(2)}) collective-permute-start(bf16[336,512]{1,0:T(8,128)(2,1)S(1)} %slice.41), channel_id=1, source_target_pairs={{0,8},{2,10},{8,16},{10,18},{12,4},{14,6},{16,24},{18,26},{20,12},... | collective-permute-start | bytes 1032200 | tf_op jit(solution)/shard_map/ppermute | solution.py:446
  35.4 3.6 %copy-start.4 = (s32[16]{0:T(128)S(1)}, s32[16]{0:T(128)}, u32[]{:S(2)}) copy-start(s32[16]{0:T(128)} %lengths.7) | copy-start | bytes 196
  35.4 13.8 %collective-permute-start.4 = (bf16[368,512]{1,0:T(8,128)(2,1)S(1)}, bf16[368,512]{1,0:T(8,128)(2,1)S(1)}, u32[]{:S(2)}, u32[]{:S(2)}) collective-permute-start(bf16[368,512]{1,0:T(8,128)(2,1)S(1)} %slice.42), channel_id=1, source_target_pairs={{0,8},{2,10},{8,16},{10,18},{12,4},{14,6},{16,24},{18,26},{20,12},... | collective-permute-start | bytes 1130504 | tf_op jit(solution)/shard_map/ppermute | solution.py:446
  38.9 10.3 %copy-start.6 = (bf16[320,256]{1,0:T(8,128)(2,1)S(1)}, bf16[320,256]{1,0:T(8,128)(2,1)}, u32[]{:S(2)}) copy-start(bf16[320,256]{1,0:T(8,128)(2,1)} %get-tuple-element.22.refs_7_) | copy-start | bytes 491524
  46.0 13.3 %collective-permute-start.9 = (bf16[352,256]{1,0:T(8,128)(2,1)S(1)}, bf16[352,256]{1,0:T(8,128)(2,1)S(1)}, u32[]{:S(2)}, u32[]{:S(2)}) collective-permute-start(bf16[352,256]{1,0:T(8,128)(2,1)S(1)} %get-tuple-element.25), channel_id=1, source_target_pairs={{0,4},{2,6},{4,0},{6,2},{8,12},{10,14},{12,8},{14,10},{16,20},{18,... | collective-permute-start | bytes 540680 | tf_op jit(solution)/shard_map/ppermute | solution.py:442
  46.1 13.2 %collective-permute-start.10 = (bf16[352,256]{1,0:T(8,128)(2,1)S(1)}, bf16[352,256]{1,0:T(8,128)(2,1)S(1)}, u32[]{:S(2)}, u32[]{:S(2)}) collective-permute-start(bf16[352,256]{1,0:T(8,128)(2,1)S(1)} %get-tuple-element.26), channel_id=1, source_target_pairs={{0,6},{2,4},{4,2},{6,0},{8,14},{10,12},{12,10},{14,8},{16,22},{18,... | collective-permute-start | bytes 540680 | tf_op jit(solution)/shard_map/ppermute | solution.py:442
  49.2 10.1 %copy-start = (bf16[320,1024]{1,0:T(8,128)(2,1)S(1)}, bf16[320,1024]{1,0:T(8,128)(2,1)}, u32[]{:S(2)}) copy-start(bf16[320,1024]{1,0:T(8,128)(2,1)} %refs_1_.1) | copy-start | bytes 1966084
  57.7 1.6 %copy-start.1 = (f32[31,1024]{1,0:T(8,128)S(1)}, f32[31,1024]{1,0:T(8,128)}, u32[]{:S(2)}) copy-start(f32[31,1024]{1,0:T(8,128)} %refs_4_.1) | copy-start | bytes 380932
  57.8 5.6 %collective-permute-start.6 = (bf16[352,256]{1,0:T(8,128)(2,1)S(1)}, bf16[352,256]{1,0:T(8,128)(2,1)S(1)}, u32[]{:S(2)}, u32[]{:S(2)}) collective-permute-start(bf16[352,256]{1,0:T(8,128)(2,1)S(1)} %get-tuple-element.23), channel_id=1, source_target_pairs={{0,2},{2,0},{4,6},{6,4},{8,10},{10,8},{12,14},{14,12},{16,18},{18,... | collective-permute-start | bytes 540680 | tf_op jit(solution)/shard_map/ppermute | solution.py:442
  59.4 3.9 %copy-start.3 = (f32[1024]{0:T(1024)S(1)}, f32[1024]{0:T(1024)}, u32[]{:S(2)}) copy-start(f32[1024]{0:T(1024)} %param.15) | copy-start | bytes 12292
  62.9 0.7 %copy-start.2 = (f32[1024]{0:T(1024)S(1)}, f32[1024]{0:T(1024)}, u32[]{:S(2)}) copy-start(f32[1024]{0:T(1024)} %param.14) | copy-start | bytes 12292

commit v2 on v1

--- a/solution.py
+++ b/solution.py
@@ -13,10 +13,10 @@
 EDGE = 16
 SAME = 2048.0
 TAILED = (1, GROUP - 1)
-WITH_Q = (2, 3)
+WITH_Q = (3,)
 KV_BLOCKS = GROUP + 2
-WIDTHS = (256, 512, 768, 1024)
-BLOCK_ROWS = 32
+WIDTHS = tuple(range(256, 1281, 128))
+BLOCK_ROWS = 64
 SPLIT_VMEM = 56 << 20
 ATTEND_VMEM = 24 << 20
 FINISH_VMEM = 24 << 20
@@ -216,22 +216,30 @@
         oh_q = one_hot(key_base + 2 * rows - EDGE + first, q_rows, SAME)
         oh_k = oh_buf[pl.ds(low, width), :]
         oh_both = jnp.concatenate([oh_q, oh_q], axis=0)
-        for p_at in range(0, cols, LANES):
+        def scores(p_at):
             at_cols = slice(p_at, p_at + LANES)
-            v_cols = slice(cols + p_at, cols + p_at + LANES)
             q = q_buf[pl.ds(first, q_rows), at_cols]
             k = jnp.concatenate([kv_buf[pl.ds(low, width), at_cols], oh_k], axis=1)
-            v = kv_buf[pl.ds(low, width), v_cols]
             q_both = jnp.concatenate([q * halves[0], q * halves[1]], axis=0)
             q_both = jnp.concatenate([q_both, oh_both], axis=1)
-            s = lax.dot_general(
+            return lax.dot_general(
                 q_both, k, (((1,), (1,)), ((), ())), preferred_element_type=jnp.float32
             )
+
+        def weigh(s, p_at):
             p = jnp.exp(s - jnp.max(s, axis=1, keepdims=True))
-            denom = jnp.sum(p, axis=1, keepdims=True)
-            o = jnp.dot(p.astype(jnp.bfloat16), v, preferred_element_type=jnp.float32) / denom
+            return p.astype(jnp.bfloat16), jnp.sum(p, axis=1, keepdims=True)
+
+        def combine(p, denom, p_at):
+            v = kv_buf[pl.ds(low, width), cols + p_at : cols + p_at + LANES]
+            o = jnp.dot(p, v, preferred_element_type=jnp.float32) / denom
             ctx = jnp.where(lane < HD, o[:q_rows], o[q_rows:])
-            ctx_buf[m, pl.ds(at, q_rows), at_cols] = ctx.astype(jnp.bfloat16)
+            ctx_buf[m, pl.ds(at, q_rows), p_at : p_at + LANES] = ctx.astype(jnp.bfloat16)
+
+        pairs = range(0, cols, LANES)
+        got = [scores(p_at) for p_at in pairs]
+        for p_at, s in zip(pairs, got):
+            combine(*weigh(s, p_at), p_at)
 
     @pl.loop(0, 2 * blocks)
     def _(t):
@@ -371,9 +379,11 @@
                 cols = pl.ds(pl.multiple_of((which[m] * per + t) * LANES, LANES), LANES)
                 sources.append((mixed, conv, i * per + t, cols))
 
-    @pl.loop(0, rows // block_rows)
+    norm_rows = rows // 2
+
+    @pl.loop(0, 2)
     def _(b):
-        at = pl.ds(pl.multiple_of(b * block_rows, 16), block_rows)
+        at = pl.ds(pl.multiple_of(b * norm_rows, 16), norm_rows)
         values = [conv[slot, at, :] for _, conv, slot, _ in sources]
         mean = jnp.sum(sum(values), axis=1, keepdims=True) / width
         centred = [x - mean for x in values]
@@ -450,12 +460,17 @@
 
     kv, q_alone = split_columns(query, key, value, residual)
     kv_group = [kv[0]] + [swap(kv[m], m) for m in range(1, GROUP)]
-    q_near = [swap(q_alone[1], 1), q_alone[0]]
+    q_1, q_2, kv_group[1] = lax.optimization_barrier((*q_alone[1:], kv_group[1]))
+    q_2 = swap(q_2, 2)
+    q_1, kv_group[2] = lax.optimization_barrier((q_1, kv_group[2]))
+    q_near = [swap(q_1, 1), q_alone[0]]
     bare = [part[: rows + EDGE + tail_rows(m)] for m, part in enumerate(kv_group)]
-    kv_halo = [move(bare[m], near if m < 2 else far) for m in range(GROUP)]
-
-    q_at = tuple(rows + EDGE + tail_rows(m) for m in (3, 2))
-    far_q = [kv_group[3], kv_group[2]]
+    kv_halo = [move(bare[m], near) for m in range(2)]
+    both = move(jnp.concatenate(bare[2:], axis=0), far)
+    kv_halo += [both[: bare[2].shape[0]], both[bare[2].shape[0] :]]
+
+    q_at = (rows + EDGE + tail_rows(3), None)
+    far_q = [kv_group[3], q_2]
     ctx_far = attend(rows, cols, (3, 2), q_at, lengths, kv_group + kv_halo[:2], far_q)
     ctx_3, ctx_2 = swap(ctx_far[0], 3), swap(ctx_far[1], 2)
     ctx_near = attend(rows, cols, (1, 0), (None, None), lengths, kv_group + kv_halo[2:], q_near)

time: 69.5 us -> 62.6 us (0.901); the launches traced: 68.6 us -> 62.4 us
  starting transfers between devices: 20.7 us -> 17 us
  Pallas kernels: 26.7 us -> 25.1 us
  waiting for transfers between devices: 20.6 us -> 19.7 us
    ppermute x4 -> x3, starting transfers between devices: 9.68 us -> 6.09 us  [move(): lax.ppermute(array, 'seq', [(i, j) for i, j in pairs if 0 <= j < peers])]
    pallas_call x1, Pallas kernels: 5.03 us -> 3.56 us  [finish(): pl.pallas_call(functools.partial(finish_kernel, BLOCK_ROWS, ms, early), o...]
    ppermute x7 -> x8, waiting for transfers between devices: 20.4 us -> 19.2 us  [swap(): return lax.ppermute(array, 'seq', [(i, i ^ m) for i in range(peers)])]
    ppermute x7 -> x8, starting transfers between devices: 11.1 us -> 11 us  [swap(): return lax.ppermute(array, 'seq', [(i, i ^ m) for i in range(peers)])]
  transfers between devices with their start and end apart: 11 -> 11, of which waited for: 4 -> 4; matrix products, arithmetic and copies ran while one was open for 0% -> 0% of each run, Pallas kernels for 28% -> 30%
where the time goes in v2:
time: 62.6 us; the launch traced here: 62.4 us
  Pallas kernels  25.1 us (40%)
  waiting for transfers between devices  19.7 us (31%)
  starting transfers between devices  17 us (27%)
    ppermute x8, waiting for transfers between devices, swap(): return lax.ppermute(array, 'seq', [(i, i ^ m) for i in range(peers)])  19.2 us
    pallas_call x2, Pallas kernels, attend(): pl.pallas_call(functools.partial(attend_kernel, rows, q_rows, widths, ms,...  15.2 us
    ppermute x8, starting transfers between devices, swap(): return lax.ppermute(array, 'seq', [(i, i ^ m) for i in range(peers)])  11 us
    ppermute x3, starting transfers between devices, move(): lax.ppermute(array, 'seq', [(i, j) for i, j in pairs if 0 <= j < peers])  6.09 us
    pallas_call x1, Pallas kernels, convolve_early(): pl.pallas_call(functools.partial(convolve_kernel, BLOCK_ROWS, ms), out_sh...  3.69 us
    pallas_call x1, Pallas kernels, finish(): pl.pallas_call(functools.partial(finish_kernel, BLOCK_ROWS, ms, early), o...  3.56 us
    pallas_call x1, Pallas kernels, split_columns(): pl.pallas_call(functools.partial(split_kernel, cols), out_shape=[jax.Shap...  2.63 us
  transfers between devices with their start and end apart: 11, of which 4 were waited for; matrix products, arithmetic and copies ran while one was open for 0% of the time, Pallas kernels for 30%

profile of v2, /device:TPU:0, one launch (start us, length us, event | category | flops | bytes accessed | tf_op | source)
XLA Modules:
  0.0 62.4 jit_solution(6597359646499747108)
XLA Ops:
  0.0 2.6 %split_columns.1 = (bf16[336,512]{1,0:T(8,128)(2,1)}, bf16[368,512]{1,0:T(8,128)(2,1)}, bf16[336,512]{1,0:T(8,128)(2,1)}, bf16[528,512]{1,0:T(8,128)(2,1)}, bf16...) custom-call(bf16[320,1024]{1,0:T(8,128)(2,1)} %query.1, bf16[320,1024]{1,0:T(8,128)(2,1)} %key.1, ...), custom_call_target="tpu_custom_call" | custom-call | tf_op jit(solution)/shard_map/split_columns/pallas_call | solution.py:109
  2.6 3.0 %collective-permute-start = (bf16[368,512]{1,0:T(8,128)(2,1)}, bf16[368,512]{1,0:T(8,128)(2,1)S(1)}, u32[]{:S(2)}, u32[]{:S(2)}) collective-permute-start(bf16[368,512]{1,0:T(8,128)(2,1)} %get-tuple-element.26), channel_id=1, source_target_pairs={{0,2},{2,0},{4,6},{6,4},{8,10},{10,8},{12,14},{14,12},{16,18},{18,... | collective-permute-start | bytes 1130504 | tf_op jit(solution)/shard_map/ppermute | solution.py:452
  5.6 1.5 %collective-permute-start.2 = (bf16[528,512]{1,0:T(8,128)(2,1)}, bf16[528,512]{1,0:T(8,128)(2,1)S(1)}, u32[]{:S(2)}, u32[]{:S(2)}) collective-permute-start(bf16[528,512]{1,0:T(8,128)(2,1)} %get-tuple-element.31), channel_id=1, source_target_pairs={{0,6},{2,4},{4,2},{6,0},{8,14},{10,12},{12,10},{14,8},{16,22},{18,... | collective-permute-start | bytes 1622024 | tf_op jit(solution)/shard_map/ppermute | solution.py:452
  7.1 0.0 collective-permute-start.1
  7.2 1.3 %collective-permute-start.6 = (bf16[336,512]{1,0:T(8,128)(2,1)}, bf16[336,512]{1,0:T(8,128)(2,1)S(1)}, u32[]{:S(2)}, u32[]{:S(2)}) collective-permute-start(bf16[336,512]{1,0:T(8,128)(2,1)} %get-tuple-element.23.refs_0_), channel_id=1, source_target_pairs={{4,12},{6,14},{8,0},{10,2},{12,20},{14,22},{16,8},{18,10},{20,28},... | collective-permute-start | bytes 1032200 | tf_op jit(solution)/shard_map/ppermute | solution.py:456
  8.5 6.9 %collective-permute-done.refs_1_ = bf16[368,512]{1,0:T(8,128)(2,1)S(1)} collective-permute-done((bf16[368,512]{1,0:T(8,128)(2,1)}, bf16[368,512]{1,0:T(8,128)(2,1)S(1)}, u32[]{:S(2)}, u32[]{:S(2)}) %collective-permute-start) | collective-permute-done | bytes 376864 | tf_op jit(solution)/shard_map/ppermute | solution.py:452
  15.4 1.3 %collective-permute-start.7 = (bf16[368,512]{1,0:T(8,128)(2,1)S(1)}, bf16[368,512]{1,0:T(8,128)(2,1)S(1)}, u32[]{:S(2)}, u32[]{:S(2)}) collective-permute-start(bf16[368,512]{1,0:T(8,128)(2,1)S(1)} %collective-permute-done.refs_1_), channel_id=1, source_target_pairs={{4,12},{6,14},{8,0},{10,2},{12,20},{14,22},{16,8},{18,10},{20,28},... | collective-permute-start | bytes 1130504 | tf_op jit(solution)/shard_map/ppermute | solution.py:456
  16.7 0.0 copy-start.4
  16.8 12.0 %collective-permute-done.1.refs_2_ = bf16[336,512]{1,0:T(8,128)(2,1)S(1)} collective-permute-done((bf16[336,512]{1,0:T(8,128)(2,1)}, bf16[336,512]{1,0:T(8,128)(2,1)S(1)}, u32[]{:S(2)}, u32[]{:S(2)}) %collective-permute-start.1) | collective-permute-done | bytes 344096 | tf_op jit(solution)/shard_map/ppermute | solution.py:452
  28.8 0.4 collective-permute-start.8
  29.2 1.6 %collective-permute-start.4 = (bf16[320,256]{1,0:T(8,128)(2,1)}, bf16[320,256]{1,0:T(8,128)(2,1)S(1)}, u32[]{:S(2)}, u32[]{:S(2)}) collective-permute-start(bf16[320,256]{1,0:T(8,128)(2,1)} %get-tuple-element.32), channel_id=1, source_target_pairs={{0,2},{2,0},{4,6},{6,4},{8,10},{10,8},{12,14},{14,12},{16,18},{18,... | collective-permute-start | bytes 491528 | tf_op jit(solution)/shard_map/ppermute | solution.py:452
  30.9 3.5 %collective-permute-start.3 = (bf16[704,512]{1,0:T(8,128)(2,1)S(1)}, bf16[704,512]{1,0:T(8,128)(2,1)S(1)}, u32[]{:S(2)}, u32[]{:S(2)}) collective-permute-start(bf16[704,512]{1,0:T(8,128)(2,1)S(1)} %pad_maximum_fusion), channel_id=1, source_target_pairs={{0,8},{2,10},{8,16},{10,18},{12,4},{14,6},{16,24},{18,26},{20,12},... | collective-permute-start | bytes 2162696 | tf_op jit(solution)/shard_map/ppermute | solution.py:456
  34.5 7.6 %attend.3 = (bf16[352,256]{1,0:T(8,128)(2,1)S(1)}, bf16[352,256]{1,0:T(8,128)(2,1)S(1)}) custom-call(s32[16]{0:T(128)S(1)} %copy-done.4, bf16[336,512]{1,0:T(8,128)(2,1)S(1)} %copy-done.5, bf16[368,512]{1,0:T(8,128)(2,1)S(1)} %collective-permute-done.refs_1_, bf16[336,512]{1,0:T(8,128)(2,1)S(1)} %collective-permute-done.1.refs_2_, ...), custom_call_target="tpu_custom_call" | custom-call | flops 5536481280 | bytes 3932160 | tf_op jit(solution)/shard_map/attend/pallas_call | solution.py:274
  42.1 0.9 %collective-permute-start.10 = (bf16[352,256]{1,0:T(8,128)(2,1)S(1)}, bf16[352,256]{1,0:T(8,128)(2,1)S(1)}, u32[]{:S(2)}, u32[]{:S(2)}) collective-permute-start(bf16[352,256]{1,0:T(8,128)(2,1)S(1)} %get-tuple-element.38), channel_id=1, source_target_pairs={{0,6},{2,4},{4,2},{6,0},{8,14},{10,12},{12,10},{14,8},{16,22},{18,... | collective-permute-start | bytes 540680 | tf_op jit(solution)/shard_map/ppermute | solution.py:452
  43.0 2.0 %collective-permute-start.9 = (bf16[352,256]{1,0:T(8,128)(2,1)S(1)}, bf16[352,256]{1,0:T(8,128)(2,1)S(1)}, u32[]{:S(2)}, u32[]{:S(2)}) collective-permute-start(bf16[352,256]{1,0:T(8,128)(2,1)S(1)} %get-tuple-element.37), channel_id=1, source_target_pairs={{0,4},{2,6},{4,0},{6,2},{8,12},{10,14},{12,8},{14,10},{16,20},{18,... | collective-permute-start | bytes 540680 | tf_op jit(solution)/shard_map/ppermute | solution.py:452
  45.0 0.5 collective-permute-done.3
  45.6 0.0 copy-start
  45.6 0.0 copy-start.1
  45.6 7.6 %attend.2 = (bf16[352,256]{1,0:T(8,128)(2,1)S(1)}, bf16[352,256]{1,0:T(8,128)(2,1)S(1)}) custom-call(s32[16]{0:T(128)S(1)} %copy-done.4, bf16[336,512]{1,0:T(8,128)(2,1)S(1)} %copy-done.5, bf16[368,512]{1,0:T(8,128)(2,1)S(1)} %collective-permute-done.refs_1_, bf16[336,512]{1,0:T(8,128)(2,1)S(1)} %collective-permute-done.1.refs_2_, ...), custom_call_target="tpu_custom_call" | custom-call | flops 5536481280 | bytes 3932160 | tf_op jit(solution)/shard_map/attend/pallas_call | solution.py:274
  53.3 1.6 %collective-permute-start.5 = (bf16[352,256]{1,0:T(8,128)(2,1)S(1)}, bf16[352,256]{1,0:T(8,128)(2,1)S(1)}, u32[]{:S(2)}, u32[]{:S(2)}) collective-permute-start(bf16[352,256]{1,0:T(8,128)(2,1)S(1)} %get-tuple-element.34), channel_id=1, source_target_pairs={{0,2},{2,0},{4,6},{6,4},{8,10},{10,8},{12,14},{14,12},{16,18},{18,... | collective-permute-start | bytes 540680 | tf_op jit(solution)/shard_map/ppermute | solution.py:452
  54.9 0.0 copy-start.3
  54.9 3.7 %convolve.1 = (bf16[6,320,128]{2,1,0:T(8,128)(2,1)S(1)}, f32[6,320,128]{2,1,0:T(8,128)S(1)}) custom-call(s32[16]{0:T(128)S(1)} %copy-done.4, bf16[352,256]{1,0:T(8,128)(2,1)S(1)} %get-tuple-element.35.refs_0_, bf16[352,256]{1,0:T(8,128)(2,1)S(1)} %collective-permute-done.9.refs_1_, bf16[352,256]{1,0:T(8,128)(2,1)S(1)} %collective-permute-done.10.refs_2_, ...), custom_call_target="tpu_custom_call" | custom-call | flops 761856000 | bytes 2621440 | tf_op jit(solution)/shard_map/convolve/pallas_call | solution.py:411
  58.6 0.2 collective-permute-done.5.refs_0_
  58.8 3.6 %finish.1 = bf16[320,1024]{1,0:T(8,128)(2,1)} custom-call(s32[16]{0:T(128)S(1)} %copy-done.4, bf16[352,256]{1,0:T(8,128)(2,1)S(1)} %collective-permute-done.5.refs_0_, bf16[320,1024]{1,0:T(8,128)(2,1)S(1)} %copy-done, bf16[16,1024]{1,0:T(8,128)(2,1)S(1)} %get-tuple-element.48.refs_4_.refs_2_, bf16[16,1024]{1,0:T(8,128)(2,1)S(1)} %get-tuple-element.47.refs_5_.refs_3_, ...), custom_call_target="tpu_custom_call" | custom-call | tf_op jit(solution)/shard_map/finish/pallas_call | solution.py:431
  (25 shorter events, 0.2 us)
Async XLA Ops:
  2.6 12.8 %collective-permute-start = (bf16[368,512]{1,0:T(8,128)(2,1)}, bf16[368,512]{1,0:T(8,128)(2,1)S(1)}, u32[]{:S(2)}, u32[]{:S(2)}) collective-permute-start(bf16[368,512]{1,0:T(8,128)(2,1)} %get-tuple-element.26), channel_id=1, source_target_pairs={{0,2},{2,0},{4,6},{6,4},{8,10},{10,8},{12,14},{14,12},{16,18},{18,... | collective-permute-start | bytes 1130504 | tf_op jit(solution)/shard_map/ppermute | solution.py:452
  5.6 25.1 %collective-permute-start.2 = (bf16[528,512]{1,0:T(8,128)(2,1)}, bf16[528,512]{1,0:T(8,128)(2,1)S(1)}, u32[]{:S(2)}, u32[]{:S(2)}) collective-permute-start(bf16[528,512]{1,0:T(8,128)(2,1)} %get-tuple-element.31), channel_id=1, source_target_pairs={{0,6},{2,4},{4,2},{6,0},{8,14},{10,12},{12,10},{14,8},{16,22},{18,... | collective-permute-start | bytes 1622024 | tf_op jit(solution)/shard_map/ppermute | solution.py:452
  7.1 21.6 %collective-permute-start.1 = (bf16[336,512]{1,0:T(8,128)(2,1)}, bf16[336,512]{1,0:T(8,128)(2,1)S(1)}, u32[]{:S(2)}, u32[]{:S(2)}) collective-permute-start(bf16[336,512]{1,0:T(8,128)(2,1)} %get-tuple-element.29), channel_id=1, source_target_pairs={{0,4},{2,6},{4,0},{6,2},{8,12},{10,14},{12,8},{14,10},{16,20},{18,... | collective-permute-start | bytes 1032200 | tf_op jit(solution)/shard_map/ppermute | solution.py:452
  7.2 27.2 %collective-permute-start.6 = (bf16[336,512]{1,0:T(8,128)(2,1)}, bf16[336,512]{1,0:T(8,128)(2,1)S(1)}, u32[]{:S(2)}, u32[]{:S(2)}) collective-permute-start(bf16[336,512]{1,0:T(8,128)(2,1)} %get-tuple-element.23.refs_0_), channel_id=1, source_target_pairs={{4,12},{6,14},{8,0},{10,2},{12,20},{14,22},{16,8},{18,10},{20,28},... | collective-permute-start | bytes 1032200 | tf_op jit(solution)/shard_map/ppermute | solution.py:456
  15.4 19.0 %collective-permute-start.7 = (bf16[368,512]{1,0:T(8,128)(2,1)S(1)}, bf16[368,512]{1,0:T(8,128)(2,1)S(1)}, u32[]{:S(2)}, u32[]{:S(2)}) collective-permute-start(bf16[368,512]{1,0:T(8,128)(2,1)S(1)} %collective-permute-done.refs_1_), channel_id=1, source_target_pairs={{4,12},{6,14},{8,0},{10,2},{12,20},{14,22},{16,8},{18,10},{20,28},... | collective-permute-start | bytes 1130504 | tf_op jit(solution)/shard_map/ppermute | solution.py:456
  16.7 17.7 %copy-start.4 = (s32[16]{0:T(128)S(1)}, s32[16]{0:T(128)}, u32[]{:S(2)}) copy-start(s32[16]{0:T(128)} %lengths.7) | copy-start | bytes 196
  16.8 17.7 %copy-start.5 = (bf16[336,512]{1,0:T(8,128)(2,1)S(1)}, bf16[336,512]{1,0:T(8,128)(2,1)}, u32[]{:S(2)}) copy-start(bf16[336,512]{1,0:T(8,128)(2,1)} %get-tuple-element.23.refs_0_) | copy-start | bytes 1032196
  28.8 5.6 %collective-permute-start.8 = (bf16[320,256]{1,0:T(8,128)(2,1)}, bf16[320,256]{1,0:T(8,128)(2,1)S(1)}, u32[]{:S(2)}, u32[]{:S(2)}) collective-permute-start(bf16[320,256]{1,0:T(8,128)(2,1)} %get-tuple-element.36), channel_id=1, source_target_pairs={{0,4},{2,6},{4,0},{6,2},{8,12},{10,14},{12,8},{14,10},{16,20},{18,... | collective-permute-start | bytes 491528 | tf_op jit(solution)/shard_map/ppermute | solution.py:452
  29.2 16.4 %collective-permute-start.4 = (bf16[320,256]{1,0:T(8,128)(2,1)}, bf16[320,256]{1,0:T(8,128)(2,1)S(1)}, u32[]{:S(2)}, u32[]{:S(2)}) collective-permute-start(bf16[320,256]{1,0:T(8,128)(2,1)} %get-tuple-element.32), channel_id=1, source_target_pairs={{0,2},{2,0},{4,6},{6,4},{8,10},{10,8},{12,14},{14,12},{16,18},{18,... | collective-permute-start | bytes 491528 | tf_op jit(solution)/shard_map/ppermute | solution.py:452
  30.9 14.7 %collective-permute-start.3 = (bf16[704,512]{1,0:T(8,128)(2,1)S(1)}, bf16[704,512]{1,0:T(8,128)(2,1)S(1)}, u32[]{:S(2)}, u32[]{:S(2)}) collective-permute-start(bf16[704,512]{1,0:T(8,128)(2,1)S(1)} %pad_maximum_fusion), channel_id=1, source_target_pairs={{0,8},{2,10},{8,16},{10,18},{12,4},{14,6},{16,24},{18,26},{20,12},... | collective-permute-start | bytes 2162696 | tf_op jit(solution)/shard_map/ppermute | solution.py:456
  42.1 3.5 %copy-start.6 = (bf16[320,256]{1,0:T(8,128)(2,1)S(1)}, bf16[320,256]{1,0:T(8,128)(2,1)}, u32[]{:S(2)}) copy-start(bf16[320,256]{1,0:T(8,128)(2,1)} %get-tuple-element.33.refs_7_) | copy-start | bytes 491524
  42.1 12.7 %collective-permute-start.10 = (bf16[352,256]{1,0:T(8,128)(2,1)S(1)}, bf16[352,256]{1,0:T(8,128)(2,1)S(1)}, u32[]{:S(2)}, u32[]{:S(2)}) collective-permute-start(bf16[352,256]{1,0:T(8,128)(2,1)S(1)} %get-tuple-element.38), channel_id=1, source_target_pairs={{0,6},{2,4},{4,2},{6,0},{8,14},{10,12},{12,10},{14,8},{16,22},{18,... | collective-permute-start | bytes 540680 | tf_op jit(solution)/shard_map/ppermute | solution.py:452
  43.0 11.8 %collective-permute-start.9 = (bf16[352,256]{1,0:T(8,128)(2,1)S(1)}, bf16[352,256]{1,0:T(8,128)(2,1)S(1)}, u32[]{:S(2)}, u32[]{:S(2)}) collective-permute-start(bf16[352,256]{1,0:T(8,128)(2,1)S(1)} %get-tuple-element.37), channel_id=1, source_target_pairs={{0,4},{2,6},{4,0},{6,2},{8,12},{10,14},{12,8},{14,10},{16,20},{18,... | collective-permute-start | bytes 540680 | tf_op jit(solution)/shard_map/ppermute | solution.py:452
  45.6 9.2 %copy-start = (bf16[320,1024]{1,0:T(8,128)(2,1)S(1)}, bf16[320,1024]{1,0:T(8,128)(2,1)}, u32[]{:S(2)}) copy-start(bf16[320,1024]{1,0:T(8,128)(2,1)} %refs_1_.1) | copy-start | bytes 1966084
  45.6 9.2 %copy-start.1 = (f32[31,1024]{1,0:T(8,128)S(1)}, f32[31,1024]{1,0:T(8,128)}, u32[]{:S(2)}) copy-start(f32[31,1024]{1,0:T(8,128)} %refs_4_.1) | copy-start | bytes 380932
  53.3 5.6 %collective-permute-start.5 = (bf16[352,256]{1,0:T(8,128)(2,1)S(1)}, bf16[352,256]{1,0:T(8,128)(2,1)S(1)}, u32[]{:S(2)}, u32[]{:S(2)}) collective-permute-start(bf16[352,256]{1,0:T(8,128)(2,1)S(1)} %get-tuple-element.34), channel_id=1, source_target_pairs={{0,2},{2,0},{4,6},{6,4},{8,10},{10,8},{12,14},{14,12},{16,18},{18,... | collective-permute-start | bytes 540680 | tf_op jit(solution)/shard_map/ppermute | solution.py:452
  54.9 3.9 %copy-start.2 = (f32[1024]{0:T(1024)S(1)}, f32[1024]{0:T(1024)}, u32[]{:S(2)}) copy-start(f32[1024]{0:T(1024)} %param.14) | copy-start | bytes 12292
  54.9 3.9 %copy-start.3 = (f32[1024]{0:T(1024)S(1)}, f32[1024]{0:T(1024)}, u32[]{:S(2)}) copy-start(f32[1024]{0:T(1024)} %param.15) | copy-start | bytes 12292

commit v3 on v2

--- a/solution.py
+++ b/solution.py
@@ -13,7 +13,7 @@
 EDGE = 16
 SAME = 2048.0
 TAILED = (1, GROUP - 1)
-WITH_Q = (3,)
+WITH_Q = ()
 KV_BLOCKS = GROUP + 2
 WIDTHS = tuple(range(256, 1281, 128))
 BLOCK_ROWS = 64
@@ -460,17 +460,17 @@
 
     kv, q_alone = split_columns(query, key, value, residual)
     kv_group = [kv[0]] + [swap(kv[m], m) for m in range(1, GROUP)]
-    q_1, q_2, kv_group[1] = lax.optimization_barrier((*q_alone[1:], kv_group[1]))
-    q_2 = swap(q_2, 2)
-    q_1, kv_group[2] = lax.optimization_barrier((q_1, kv_group[2]))
+    q_2, q_3, kv_group[1] = lax.optimization_barrier((*q_alone[2:], kv_group[1]))
+    q_3, q_2 = swap(q_3, 3), swap(q_2, 2)
+    q_1, kv_group[3] = lax.optimization_barrier((q_alone[1], kv_group[3]))
     q_near = [swap(q_1, 1), q_alone[0]]
     bare = [part[: rows + EDGE + tail_rows(m)] for m, part in enumerate(kv_group)]
     kv_halo = [move(bare[m], near) for m in range(2)]
     both = move(jnp.concatenate(bare[2:], axis=0), far)
     kv_halo += [both[: bare[2].shape[0]], both[bare[2].shape[0] :]]
 
-    q_at = (rows + EDGE + tail_rows(3), None)
-    far_q = [kv_group[3], q_2]
+    q_at = (None, None)
+    far_q = [q_3, q_2]
     ctx_far = attend(rows, cols, (3, 2), q_at, lengths, kv_group + kv_halo[:2], far_q)
     ctx_3, ctx_2 = swap(ctx_far[0], 3), swap(ctx_far[1], 2)
     ctx_near = attend(rows, cols, (1, 0), (None, None), lengths, kv_group + kv_halo[2:], q_near)

time: 62.6 us -> 60.3 us (0.963)
  the two profiles are of different devices: /device:TPU:0 before, /device:TPU:16 now
where the time goes in v3:
time: 60.3 us; the launch traced here: 60.4 us
  Pallas kernels  26.5 us (44%)
  starting transfers between devices  21 us (35%)
  waiting for transfers between devices  12.4 us (21%)
    pallas_call x2, Pallas kernels, attend(): pl.pallas_call(functools.partial(attend_kernel, rows, q_rows, widths, ms,...  16.5 us
    ppermute x9, starting transfers between devices, swap(): return lax.ppermute(array, 'seq', [(i, i ^ m) for i in range(peers)])  12.9 us
    ppermute x9, waiting for transfers between devices, swap(): return lax.ppermute(array, 'seq', [(i, i ^ m) for i in range(peers)])  12.4 us
    ppermute x3, starting transfers between devices, move(): lax.ppermute(array, 'seq', [(i, j) for i, j in pairs if 0 <= j < peers])  8.18 us
    pallas_call x1, Pallas kernels, convolve_early(): pl.pallas_call(functools.partial(convolve_kernel, BLOCK_ROWS, ms), out_sh...  3.75 us
    pallas_call x1, Pallas kernels, finish(): pl.pallas_call(functools.partial(finish_kernel, BLOCK_ROWS, ms, early), o...  3.63 us
    pallas_call x1, Pallas kernels, split_columns(): pl.pallas_call(functools.partial(split_kernel, cols), out_shape=[jax.Shap...  2.62 us
  transfers between devices with their start and end apart: 12, of which 4 were waited for; matrix products, arithmetic and copies ran while one was open for 0% of the time, Pallas kernels for 34%

profile of v3, /device:TPU:16, one launch (start us, length us, event | category | flops | bytes accessed | tf_op | source)
XLA Modules:
  0.0 60.4 jit_solution(292808877215353507)
XLA Ops:
  0.0 2.6 %split_columns.1 = (bf16[336,512]{1,0:T(8,128)(2,1)}, bf16[368,512]{1,0:T(8,128)(2,1)}, bf16[336,512]{1,0:T(8,128)(2,1)}, bf16[368,512]{1,0:T(8,128)(2,1)}, bf16...) custom-call(bf16[320,1024]{1,0:T(8,128)(2,1)} %query.1, ...), custom_call_target="tpu_custom_call" | custom-call | tf_op jit(solution)/shard_map/split_columns/pallas_call | solution.py:109
  2.6 0.0 copy-start.4
  2.7 1.6 %collective-permute-start = (bf16[368,512]{1,0:T(8,128)(2,1)}, bf16[368,512]{1,0:T(8,128)(2,1)S(1)}, u32[]{:S(2)}, u32[]{:S(2)}) collective-permute-start(bf16[368,512]{1,0:T(8,128)(2,1)} %get-tuple-element.27), channel_id=1, source_target_pairs={{0,2},{2,0},{4,6},{6,4},{8,10},{10,8},{12,14},{14,12},{16,18},{18,... | collective-permute-start | bytes 1130504 | tf_op jit(solution)/shard_map/ppermute | solution.py:452
  4.2 1.5 %collective-permute-start.2 = (bf16[368,512]{1,0:T(8,128)(2,1)}, bf16[368,512]{1,0:T(8,128)(2,1)S(1)}, u32[]{:S(2)}, u32[]{:S(2)}) collective-permute-start(bf16[368,512]{1,0:T(8,128)(2,1)} %get-tuple-element.31), channel_id=1, source_target_pairs={{0,6},{2,4},{4,2},{6,0},{8,14},{10,12},{12,10},{14,8},{16,22},{18,... | collective-permute-start | bytes 1130504 | tf_op jit(solution)/shard_map/ppermute | solution.py:452
  5.7 0.5 collective-permute-start.1
  6.2 2.3 %collective-permute-start.6 = (bf16[336,512]{1,0:T(8,128)(2,1)}, bf16[336,512]{1,0:T(8,128)(2,1)S(1)}, u32[]{:S(2)}, u32[]{:S(2)}) collective-permute-start(bf16[336,512]{1,0:T(8,128)(2,1)} %get-tuple-element.24.refs_0_), channel_id=1, source_target_pairs={{4,12},{6,14},{8,0},{10,2},{12,20},{14,22},{16,8},{18,10},{20,28},... | collective-permute-start | bytes 1032200 | tf_op jit(solution)/shard_map/ppermute | solution.py:456
  8.6 6.0 %collective-permute-done.refs_1_ = bf16[368,512]{1,0:T(8,128)(2,1)S(1)} collective-permute-done((bf16[368,512]{1,0:T(8,128)(2,1)}, bf16[368,512]{1,0:T(8,128)(2,1)S(1)}, u32[]{:S(2)}, u32[]{:S(2)}) %collective-permute-start) | collective-permute-done | bytes 376864 | tf_op jit(solution)/shard_map/ppermute | solution.py:452
  14.6 2.3 %collective-permute-start.7 = (bf16[368,512]{1,0:T(8,128)(2,1)S(1)}, bf16[368,512]{1,0:T(8,128)(2,1)S(1)}, u32[]{:S(2)}, u32[]{:S(2)}) collective-permute-start(bf16[368,512]{1,0:T(8,128)(2,1)S(1)} %collective-permute-done.refs_1_), channel_id=1, source_target_pairs={{4,12},{6,14},{8,0},{10,2},{12,20},{14,22},{16,8},{18,10},{20,28},... | collective-permute-start | bytes 1130504 | tf_op jit(solution)/shard_map/ppermute | solution.py:456
  16.9 3.6 %collective-permute-start.8 = (bf16[320,256]{1,0:T(8,128)(2,1)}, bf16[320,256]{1,0:T(8,128)(2,1)S(1)}, u32[]{:S(2)}, u32[]{:S(2)}) collective-permute-start(bf16[320,256]{1,0:T(8,128)(2,1)} %get-tuple-element.37), channel_id=1, source_target_pairs={{0,6},{2,4},{4,2},{6,0},{8,14},{10,12},{12,10},{14,8},{16,22},{18,... | collective-permute-start | bytes 491528 | tf_op jit(solution)/shard_map/ppermute | solution.py:452
  20.6 3.1 %collective-permute-done.2.refs_3_ = bf16[368,512]{1,0:T(8,128)(2,1)S(1)} collective-permute-done((bf16[368,512]{1,0:T(8,128)(2,1)}, bf16[368,512]{1,0:T(8,128)(2,1)S(1)}, u32[]{:S(2)}, u32[]{:S(2)}) %collective-permute-start.2) | collective-permute-done | bytes 376864 | tf_op jit(solution)/shard_map/ppermute | solution.py:452
  23.7 0.5 collective-permute-start.9
  24.2 3.1 %collective-permute-done.1.refs_2_ = bf16[336,512]{1,0:T(8,128)(2,1)S(1)} collective-permute-done((bf16[336,512]{1,0:T(8,128)(2,1)}, bf16[336,512]{1,0:T(8,128)(2,1)S(1)}, u32[]{:S(2)}, u32[]{:S(2)}) %collective-permute-start.1) | collective-permute-done | bytes 344096 | tf_op jit(solution)/shard_map/ppermute | solution.py:452
  27.4 3.5 %collective-permute-start.3 = (bf16[704,512]{1,0:T(8,128)(2,1)S(1)}, bf16[704,512]{1,0:T(8,128)(2,1)S(1)}, u32[]{:S(2)}, u32[]{:S(2)}) collective-permute-start(bf16[704,512]{1,0:T(8,128)(2,1)S(1)} %pad_maximum_fusion), channel_id=1, source_target_pairs={{0,8},{2,10},{8,16},{10,18},{12,4},{14,6},{16,24},{18,26},{20,12},... | collective-permute-start | bytes 2162696 | tf_op jit(solution)/shard_map/ppermute | solution.py:456
  30.9 1.6 %collective-permute-start.4 = (bf16[320,256]{1,0:T(8,128)(2,1)S(1)}, bf16[320,256]{1,0:T(8,128)(2,1)S(1)}, u32[]{:S(2)}, u32[]{:S(2)}) collective-permute-start(bf16[320,256]{1,0:T(8,128)(2,1)S(1)} %copy-done.7), channel_id=1, source_target_pairs={{0,2},{2,0},{4,6},{6,4},{8,10},{10,8},{12,14},{14,12},{16,18},{18,... | collective-permute-start | bytes 491528 | tf_op jit(solution)/shard_map/ppermute | solution.py:452
  32.5 8.0 %attend.3 = (bf16[352,256]{1,0:T(8,128)(2,1)S(1)}, bf16[352,256]{1,0:T(8,128)(2,1)S(1)}) custom-call(s32[16]{0:T(128)S(1)} %copy-done.4, bf16[336,512]{1,0:T(8,128)(2,1)S(1)} %copy-done.5, bf16[368,512]{1,0:T(8,128)(2,1)S(1)} %collective-permute-done.refs_1_, bf16[336,512]{1,0:T(8,128)(2,1)S(1)} %collective-permute-done.1.refs_2_, ...), custom_call_target="tpu_custom_call" | custom-call | flops 5536481280 | bytes 3932160 | tf_op jit(solution)/shard_map/attend/pallas_call | solution.py:274
  40.5 0.1 collective-permute-start.10
  40.6 2.0 %collective-permute-start.11 = (bf16[352,256]{1,0:T(8,128)(2,1)S(1)}, bf16[352,256]{1,0:T(8,128)(2,1)S(1)}, u32[]{:S(2)}, u32[]{:S(2)}) collective-permute-start(bf16[352,256]{1,0:T(8,128)(2,1)S(1)} %get-tuple-element.40), channel_id=1, source_target_pairs={{0,6},{2,4},{4,2},{6,0},{8,14},{10,12},{12,10},{14,8},{16,22},{18,... | collective-permute-start | bytes 540680 | tf_op jit(solution)/shard_map/ppermute | solution.py:452
  42.6 0.0 copy-start
  42.7 8.5 %attend.2 = (bf16[352,256]{1,0:T(8,128)(2,1)S(1)}, bf16[352,256]{1,0:T(8,128)(2,1)S(1)}) custom-call(s32[16]{0:T(128)S(1)} %copy-done.4, bf16[336,512]{1,0:T(8,128)(2,1)S(1)} %copy-done.5, bf16[368,512]{1,0:T(8,128)(2,1)S(1)} %collective-permute-done.refs_1_, bf16[336,512]{1,0:T(8,128)(2,1)S(1)} %collective-permute-done.1.refs_2_, ...), custom_call_target="tpu_custom_call" | custom-call | flops 5536481280 | bytes 3932160 | tf_op jit(solution)/shard_map/attend/pallas_call | solution.py:274
  51.2 1.5 %collective-permute-start.5 = (bf16[352,256]{1,0:T(8,128)(2,1)S(1)}, bf16[352,256]{1,0:T(8,128)(2,1)S(1)}, u32[]{:S(2)}, u32[]{:S(2)}) collective-permute-start(bf16[352,256]{1,0:T(8,128)(2,1)S(1)} %get-tuple-element.35), channel_id=1, source_target_pairs={{0,2},{2,0},{4,6},{6,4},{8,10},{10,8},{12,14},{14,12},{16,18},{18,... | collective-permute-start | bytes 540680 | tf_op jit(solution)/shard_map/ppermute | solution.py:452
  52.8 0.0 copy-start.2
  52.8 3.8 %convolve.1 = (bf16[6,320,128]{2,1,0:T(8,128)(2,1)S(1)}, f32[6,320,128]{2,1,0:T(8,128)S(1)}) custom-call(s32[16]{0:T(128)S(1)} %copy-done.4, bf16[352,256]{1,0:T(8,128)(2,1)S(1)} %get-tuple-element.36.refs_0_, bf16[352,256]{1,0:T(8,128)(2,1)S(1)} %collective-permute-done.10.refs_1_, bf16[352,256]{1,0:T(8,128)(2,1)S(1)} %collective-permute-done.11.refs_2_, ...), custom_call_target="tpu_custom_call" | custom-call | flops 761856000 | bytes 2621440 | tf_op jit(solution)/shard_map/convolve/pallas_call | solution.py:411
  56.6 0.2 collective-permute-done.5.refs_0_
  56.8 3.6 %finish.1 = bf16[320,1024]{1,0:T(8,128)(2,1)} custom-call(s32[16]{0:T(128)S(1)} %copy-done.4, bf16[352,256]{1,0:T(8,128)(2,1)S(1)} %collective-permute-done.5.refs_0_, bf16[320,1024]{1,0:T(8,128)(2,1)S(1)} %copy-done, bf16[16,1024]{1,0:T(8,128)(2,1)S(1)} %get-tuple-element.50.refs_4_.refs_2_, bf16[16,1024]{1,0:T(8,128)(2,1)S(1)} %get-tuple-element.49.refs_5_.refs_3_, ...), custom_call_target="tpu_custom_call" | custom-call | tf_op jit(solution)/shard_map/finish/pallas_call | solution.py:431
  (28 shorter events, 0.2 us)
Async XLA Ops:
  2.6 28.3 %copy-start.7 = (bf16[320,256]{1,0:T(8,128)(2,1)S(1)}, bf16[320,256]{1,0:T(8,128)(2,1)}, u32[]{:S(2)}) copy-start(bf16[320,256]{1,0:T(8,128)(2,1)} %get-tuple-element.33) | copy-start | bytes 491524
  2.6 29.9 %copy-start.4 = (s32[16]{0:T(128)S(1)}, s32[16]{0:T(128)}, u32[]{:S(2)}) copy-start(s32[16]{0:T(128)} %lengths.7) | copy-start | bytes 196
  2.6 29.9 %copy-start.5 = (bf16[336,512]{1,0:T(8,128)(2,1)S(1)}, bf16[336,512]{1,0:T(8,128)(2,1)}, u32[]{:S(2)}) copy-start(bf16[336,512]{1,0:T(8,128)(2,1)} %get-tuple-element.24.refs_0_) | copy-start | bytes 1032196
  2.7 11.9 %collective-permute-start = (bf16[368,512]{1,0:T(8,128)(2,1)}, bf16[368,512]{1,0:T(8,128)(2,1)S(1)}, u32[]{:S(2)}, u32[]{:S(2)}) collective-permute-start(bf16[368,512]{1,0:T(8,128)(2,1)} %get-tuple-element.27), channel_id=1, source_target_pairs={{0,2},{2,0},{4,6},{6,4},{8,10},{10,8},{12,14},{14,12},{16,18},{18,... | collective-permute-start | bytes 1130504 | tf_op jit(solution)/shard_map/ppermute | solution.py:452
  4.2 19.5 %collective-permute-start.2 = (bf16[368,512]{1,0:T(8,128)(2,1)}, bf16[368,512]{1,0:T(8,128)(2,1)S(1)}, u32[]{:S(2)}, u32[]{:S(2)}) collective-permute-start(bf16[368,512]{1,0:T(8,128)(2,1)} %get-tuple-element.31), channel_id=1, source_target_pairs={{0,6},{2,4},{4,2},{6,0},{8,14},{10,12},{12,10},{14,8},{16,22},{18,... | collective-permute-start | bytes 1130504 | tf_op jit(solution)/shard_map/ppermute | solution.py:452
  5.7 21.6 %collective-permute-start.1 = (bf16[336,512]{1,0:T(8,128)(2,1)}, bf16[336,512]{1,0:T(8,128)(2,1)S(1)}, u32[]{:S(2)}, u32[]{:S(2)}) collective-permute-start(bf16[336,512]{1,0:T(8,128)(2,1)} %get-tuple-element.29), channel_id=1, source_target_pairs={{0,4},{2,6},{4,0},{6,2},{8,12},{10,14},{12,8},{14,10},{16,20},{18,... | collective-permute-start | bytes 1032200 | tf_op jit(solution)/shard_map/ppermute | solution.py:452
  6.2 24.7 %collective-permute-start.6 = (bf16[336,512]{1,0:T(8,128)(2,1)}, bf16[336,512]{1,0:T(8,128)(2,1)S(1)}, u32[]{:S(2)}, u32[]{:S(2)}) collective-permute-start(bf16[336,512]{1,0:T(8,128)(2,1)} %get-tuple-element.24.refs_0_), channel_id=1, source_target_pairs={{4,12},{6,14},{8,0},{10,2},{12,20},{14,22},{16,8},{18,10},{20,28},... | collective-permute-start | bytes 1032200 | tf_op jit(solution)/shard_map/ppermute | solution.py:456
  14.6 17.9 %collective-permute-start.7 = (bf16[368,512]{1,0:T(8,128)(2,1)S(1)}, bf16[368,512]{1,0:T(8,128)(2,1)S(1)}, u32[]{:S(2)}, u32[]{:S(2)}) collective-permute-start(bf16[368,512]{1,0:T(8,128)(2,1)S(1)} %collective-permute-done.refs_1_), channel_id=1, source_target_pairs={{4,12},{6,14},{8,0},{10,2},{12,20},{14,22},{16,8},{18,10},{20,28},... | collective-permute-start | bytes 1130504 | tf_op jit(solution)/shard_map/ppermute | solution.py:456
  16.9 15.6 %collective-permute-start.8 = (bf16[320,256]{1,0:T(8,128)(2,1)}, bf16[320,256]{1,0:T(8,128)(2,1)S(1)}, u32[]{:S(2)}, u32[]{:S(2)}) collective-permute-start(bf16[320,256]{1,0:T(8,128)(2,1)} %get-tuple-element.37), channel_id=1, source_target_pairs={{0,6},{2,4},{4,2},{6,0},{8,14},{10,12},{12,10},{14,8},{16,22},{18,... | collective-permute-start | bytes 491528 | tf_op jit(solution)/shard_map/ppermute | solution.py:452
  23.7 8.8 %collective-permute-start.9 = (bf16[320,256]{1,0:T(8,128)(2,1)}, bf16[320,256]{1,0:T(8,128)(2,1)S(1)}, u32[]{:S(2)}, u32[]{:S(2)}) collective-permute-start(bf16[320,256]{1,0:T(8,128)(2,1)} %get-tuple-element.38), channel_id=1, source_target_pairs={{0,4},{2,6},{4,0},{6,2},{8,12},{10,14},{12,8},{14,10},{16,20},{18,... | collective-permute-start | bytes 491528 | tf_op jit(solution)/shard_map/ppermute | solution.py:452
  27.4 15.2 %collective-permute-start.3 = (bf16[704,512]{1,0:T(8,128)(2,1)S(1)}, bf16[704,512]{1,0:T(8,128)(2,1)S(1)}, u32[]{:S(2)}, u32[]{:S(2)}) collective-permute-start(bf16[704,512]{1,0:T(8,128)(2,1)S(1)} %pad_maximum_fusion), channel_id=1, source_target_pairs={{0,8},{2,10},{8,16},{10,18},{12,4},{14,6},{16,24},{18,26},{20,12},... | collective-permute-start | bytes 2162696 | tf_op jit(solution)/shard_map/ppermute | solution.py:456
  30.9 11.7 %collective-permute-start.4 = (bf16[320,256]{1,0:T(8,128)(2,1)S(1)}, bf16[320,256]{1,0:T(8,128)(2,1)S(1)}, u32[]{:S(2)}, u32[]{:S(2)}) collective-permute-start(bf16[320,256]{1,0:T(8,128)(2,1)S(1)} %copy-done.7), channel_id=1, source_target_pairs={{0,2},{2,0},{4,6},{6,4},{8,10},{10,8},{12,14},{14,12},{16,18},{18,... | collective-permute-start | bytes 491528 | tf_op jit(solution)/shard_map/ppermute | solution.py:452
  40.5 2.2 %copy-start.6 = (bf16[320,256]{1,0:T(8,128)(2,1)S(1)}, bf16[320,256]{1,0:T(8,128)(2,1)}, u32[]{:S(2)}) copy-start(bf16[320,256]{1,0:T(8,128)(2,1)} %get-tuple-element.34.refs_7_) | copy-start | bytes 491524
  40.5 12.3 %collective-permute-start.10 = (bf16[352,256]{1,0:T(8,128)(2,1)S(1)}, bf16[352,256]{1,0:T(8,128)(2,1)S(1)}, u32[]{:S(2)}, u32[]{:S(2)}) collective-permute-start(bf16[352,256]{1,0:T(8,128)(2,1)S(1)} %get-tuple-element.39), channel_id=1, source_target_pairs={{0,4},{2,6},{4,0},{6,2},{8,12},{10,14},{12,8},{14,10},{16,20},{18,... | collective-permute-start | bytes 540680 | tf_op jit(solution)/shard_map/ppermute | solution.py:452
  40.6 12.2 %collective-permute-start.11 = (bf16[352,256]{1,0:T(8,128)(2,1)S(1)}, bf16[352,256]{1,0:T(8,128)(2,1)S(1)}, u32[]{:S(2)}, u32[]{:S(2)}) collective-permute-start(bf16[352,256]{1,0:T(8,128)(2,1)S(1)} %get-tuple-element.40), channel_id=1, source_target_pairs={{0,6},{2,4},{4,2},{6,0},{8,14},{10,12},{12,10},{14,8},{16,22},{18,... | collective-permute-start | bytes 540680 | tf_op jit(solution)/shard_map/ppermute | solution.py:452
  42.6 10.2 %copy-start = (bf16[320,1024]{1,0:T(8,128)(2,1)S(1)}, bf16[320,1024]{1,0:T(8,128)(2,1)}, u32[]{:S(2)}) copy-start(bf16[320,1024]{1,0:T(8,128)(2,1)} %refs_1_.1) | copy-start | bytes 1966084
  42.7 10.1 %copy-start.1 = (f32[31,1024]{1,0:T(8,128)S(1)}, f32[31,1024]{1,0:T(8,128)}, u32[]{:S(2)}) copy-start(f32[31,1024]{1,0:T(8,128)} %refs_4_.1) | copy-start | bytes 380932
  51.2 5.6 %collective-permute-start.5 = (bf16[352,256]{1,0:T(8,128)(2,1)S(1)}, bf16[352,256]{1,0:T(8,128)(2,1)S(1)}, u32[]{:S(2)}, u32[]{:S(2)}) collective-permute-start(bf16[352,256]{1,0:T(8,128)(2,1)S(1)} %get-tuple-element.35), channel_id=1, source_target_pairs={{0,2},{2,0},{4,6},{6,4},{8,10},{10,8},{12,14},{14,12},{16,18},{18,... | collective-permute-start | bytes 540680 | tf_op jit(solution)/shard_map/ppermute | solution.py:452
  52.8 3.9 %copy-start.2 = (f32[1024]{0:T(1024)S(1)}, f32[1024]{0:T(1024)}, u32[]{:S(2)}) copy-start(f32[1024]{0:T(1024)} %param.14) | copy-start | bytes 12292
  52.8 3.9 %copy-start.3 = (f32[1024]{0:T(1024)S(1)}, f32[1024]{0:T(1024)}, u32[]{:S(2)}) copy-start(f32[1024]{0:T(1024)} %param.15) | copy-start | bytes 12292

commit v4 on v3

--- a/solution.py
+++ b/solution.py
@@ -12,7 +12,7 @@
 GROUP = 4
 EDGE = 16
 SAME = 2048.0
-TAILED = (1, GROUP - 1)
+TAILED = (0, 1)
 WITH_Q = ()
 KV_BLOCKS = GROUP + 2
 WIDTHS = tuple(range(256, 1281, 128))
@@ -52,10 +52,7 @@
         load.start()
     tails = [None] * GROUP
     for m in TAILED:
-        if m == 1:
-            up = which[m] > which[0]
-        else:
-            up = (which[0] == 1) | (which[0] == GROUP - 1)
+        up = which[m] > which[0] if m else which[0] % 2 == 1
         at = pl.multiple_of(jnp.where(up, rows - EDGE, 0), EDGE)
         src = residual.at[pl.ds(at, EDGE), :]
         tails[m] = pltpu.make_async_copy(src, tail.at[m], in_sem.at[6 + m])
@@ -127,8 +124,9 @@
 
 
 def attend_kernel(rows, q_rows, widths, ms, q_at, lengths, *refs):
+    ext = rows + 2 * EDGE
     kv_in, q_in, outs = refs[:KV_BLOCKS], refs[KV_BLOCKS : KV_BLOCKS + 2], refs[KV_BLOCKS + 2 : KV_BLOCKS + 4]
-    q_buf, kv_buf, oh_buf, edges, ctx_buf, q_sem, kv_sem, edge_sem, out_sem, meta = refs[
+    q_buf, kv_buf, oh_buf, edges, ctx_buf, q_sem, kv_sem, edge_sem, out_sem, tail_sem, meta = refs[
         KV_BLOCKS + 4 :
     ]
     cols = q_buf.shape[1]
@@ -160,6 +158,21 @@
     for copy in copies:
         copy.start()
 
+    def hand_on(act):
+        inner = (which[0] != 0) & (which[0] != GROUP - 1)
+        for mine, src in ((inner, kv_in[0]), (jnp.logical_not(inner), kv_in[GROUP])):
+
+            @pl.when(mine)
+            def _(src=src):
+                for i in range(4):
+                    at = pl.ds(rows + (1 + i // 2) * EDGE, EDGE)
+                    part = src.at[at, pl.ds(i % 2 * cols, cols)]
+                    dst = outs[0].at[pl.ds(ext + i * EDGE, EDGE), :]
+                    act(pltpu.make_async_copy(part, dst, tail_sem.at[i]))
+
+    if GROUP - 1 in ms:
+        hand_on(lambda copy: copy.start())
+
     utt_lane = lax.broadcasted_iota(jnp.int32, (1, oh_buf.shape[1]), 1)
     spans = []
     for m in ms:
@@ -255,11 +268,18 @@
 
             below = width
 
-    copies = [pltpu.make_async_copy(ctx_buf.at[m], outs[m], out_sem.at[m]) for m in range(2)]
-    for copy in copies:
-        copy.start()
-    for copy in copies:
-        copy.wait()
+        for i in range(2):
+
+            @pl.when(t == (i + 1) * blocks - 1)
+            def _(i=i):
+                dst = outs[i].at[pl.ds(0, ext), :]
+                pltpu.make_async_copy(ctx_buf.at[i], dst, out_sem.at[i]).start()
+
+    for i in range(2):
+        dst = outs[i].at[pl.ds(0, ext), :]
+        pltpu.make_async_copy(ctx_buf.at[i], dst, out_sem.at[i]).wait()
+    if GROUP - 1 in ms:
+        hand_on(lambda copy: copy.wait())
 
 
 def attend(rows, cols, ms, q_at, lengths, kv_parts, q_parts):
@@ -269,11 +289,14 @@
     most = -(-(q_rows + 4 * rows + 16) // LANES) * LANES
     widths = sorted({min(w, most) for w in WIDTHS + (most,)})
     utts = -(-lengths.shape[0] // LANES) * LANES
-    shape = jax.ShapeDtypeStruct((ext, cols), jnp.bfloat16)
+    shapes = [
+        jax.ShapeDtypeStruct((ext + (4 * EDGE if m == GROUP - 1 else 0), cols), jnp.bfloat16)
+        for m in ms
+    ]
     dma = pltpu.SemaphoreType.DMA
     return pl.pallas_call(
         functools.partial(attend_kernel, rows, q_rows, widths, ms, q_at),
-        out_shape=[shape] * 2,
+        out_shape=shapes,
         in_specs=[SMEM] + [ANY] * (KV_BLOCKS + 2),
         out_specs=[ANY] * 2,
         scratch_shapes=[
@@ -286,18 +309,19 @@
             dma((KV_BLOCKS,)),
             dma((KV_BLOCKS,)),
             dma((2,)),
+            dma((4,)),
             pltpu.SMEM((3, 4), jnp.int32),
         ],
         compiler_params=pltpu.CompilerParams(vmem_limit_bytes=ATTEND_VMEM),
         cost_estimate=pl.CostEstimate(
-            flops=32 * ext * cols * keys, bytes_accessed=8 * keys * cols, transcendentals=0
+            flops=64 * ext * cols * keys, bytes_accessed=8 * keys * cols, transcendentals=0
         ),
         name="attend",
     )(lengths, *kv_parts, *q_parts)
 
 
-def convolve(block_rows, ms, lengths, ctx_in, res, before, after, kernel, mixed_out, conv_out, scratch):
-    mixed, window, starts, ends = scratch
+def convolve(block_rows, ms, lengths, ctx_in, res, near_tail, other, kernel, mixed_out, conv_out, scratch):
+    mixed, window, edges, starts, ends = scratch
     rows, width = res.shape
     _, base, which = group_place(rows)
     own = base + which[0] * rows
@@ -316,6 +340,15 @@
         return end + lengths[u]
 
     lax.fori_loop(0, lengths.shape[0], note, jnp.int32(0))
+    side = which[0] % 2
+    part = width // 2
+    for i in range(2):
+        edges[1 - side, :, i * part : (i + 1) * part] = near_tail[i * EDGE : (i + 1) * EDGE, :]
+    part = width // 4
+    for i in range(4):
+        first = rows + (2 + i) * EDGE
+        edges[side, :, i * part : (i + 1) * part] = other[first : first + EDGE, :]
+    before, after = edges.at[0], edges.at[1]
     for slot, (i, t, cols) in enumerate(tiles):
         ctx = ctx_in[i][:, t * LANES : (t + 1) * LANES].astype(jnp.float32)
         for first, part in ((0, before), (EDGE, res), (EDGE + rows, after)):
@@ -358,17 +391,17 @@
 
 def convolve_kernel(block_rows, ms, lengths, *refs):
     ctx_in = refs[: len(ms)]
-    res, before, after, kernel, mixed_out, conv_out = refs[len(ms) : len(ms) + 6]
+    res, near_tail, other, kernel, mixed_out, conv_out = refs[len(ms) : len(ms) + 6]
     scratch = refs[len(ms) + 6 :]
-    convolve(block_rows, ms, lengths, ctx_in, res, before, after, kernel, mixed_out, conv_out, scratch)
+    convolve(block_rows, ms, lengths, ctx_in, res, near_tail, other, kernel, mixed_out, conv_out, scratch)
 
 
 def finish_kernel(block_rows, ms, early, lengths, *refs):
     ctx_in = refs[: len(ms)]
-    res, before, after, kernel, gain, shift, mixed_in, conv_in, out = refs[len(ms) : len(ms) + 9]
+    res, near_tail, other, kernel, gain, shift, mixed_in, conv_in, out = refs[len(ms) : len(ms) + 9]
     mixed_own, conv_own = refs[len(ms) + 9 : len(ms) + 11]
     scratch = refs[len(ms) + 11 :]
-    convolve(block_rows, ms, lengths, ctx_in, res, before, after, kernel, mixed_own, conv_own, scratch)
+    convolve(block_rows, ms, lengths, ctx_in, res, near_tail, other, kernel, mixed_own, conv_own, scratch)
     rows, width = res.shape
     _, _, which = group_place(rows)
     per = width // LANES // GROUP
@@ -391,20 +424,21 @@
         inverse = 1.0 / jnp.sqrt(var + 1e-05)
         for x, (mixed, _, slot, cols) in zip(centred, sources):
             normed = x * inverse * gain[:, cols] + shift[:, cols]
-            gated = normed * jax.nn.sigmoid(normed)
+            gated = 0.5 * normed * (1.0 + jnp.tanh(0.5 * normed))
             out[at, cols] = (mixed[slot, at, :].astype(jnp.float32) + gated).astype(jnp.bfloat16)
 
 
-def conv_scratch(slots, rows, block_rows, utts):
+def conv_scratch(slots, rows, width, block_rows, utts):
     return [
         pltpu.VMEM((slots, rows + 2 * EDGE, LANES), jnp.float32),
         pltpu.VMEM((slots, block_rows + 2 * EDGE, LANES), jnp.float32),
+        pltpu.VMEM((2, EDGE, width), jnp.bfloat16),
         pltpu.SMEM((utts,), jnp.int32),
         pltpu.SMEM((utts,), jnp.int32),
     ]
 
 
-def convolve_early(ms, lengths, ctx_parts, res, before, after, kernel):
+def convolve_early(ms, lengths, ctx_parts, res, near_tail, other, kernel):
     rows, width = res.shape
     slots = len(ms) * width // LANES // GROUP
     taps = kernel.shape[0]
@@ -416,16 +450,16 @@
         ],
         in_specs=[SMEM] + [VMEM] * (len(ms) + 4),
         out_specs=[VMEM] * 2,
-        scratch_shapes=conv_scratch(slots, rows, BLOCK_ROWS, lengths.shape[0]),
+        scratch_shapes=conv_scratch(slots, rows, width, BLOCK_ROWS, lengths.shape[0]),
         compiler_params=pltpu.CompilerParams(vmem_limit_bytes=FINISH_VMEM),
         cost_estimate=pl.CostEstimate(
             flops=100 * taps * rows * slots * LANES, bytes_accessed=8 * rows * width, transcendentals=0
         ),
         name="convolve",
-    )(lengths, *ctx_parts, res, before, after, kernel)
-
-
-def finish(ms, early, lengths, ctx_parts, res, before, after, kernel, gain, shift, mixed, conv):
+    )(lengths, *ctx_parts, res, near_tail, other, kernel)
+
+
+def finish(ms, early, lengths, ctx_parts, res, near_tail, other, kernel, gain, shift, mixed, conv):
     rows, width = res.shape
     slots = len(ms) * width // LANES // GROUP
     return pl.pallas_call(
@@ -437,10 +471,10 @@
             pltpu.VMEM((slots, rows, LANES), jnp.bfloat16),
             pltpu.VMEM((slots, rows, LANES), jnp.float32),
         ]
-        + conv_scratch(slots, rows, BLOCK_ROWS, lengths.shape[0]),
+        + conv_scratch(slots, rows, width, BLOCK_ROWS, lengths.shape[0]),
         compiler_params=pltpu.CompilerParams(vmem_limit_bytes=FINISH_VMEM),
         name="finish",
-    )(lengths, *ctx_parts, res, before, after, kernel, gain, shift, mixed, conv)
+    )(lengths, *ctx_parts, res, near_tail, other, kernel, gain, shift, mixed, conv)
 
 
 def local(query, key, value, residual, lengths, depth_kernel, gain, shift):
@@ -476,18 +510,8 @@
     ctx_near = attend(rows, cols, (1, 0), (None, None), lengths, kv_group + kv_halo[2:], q_near)
     ctx_1 = swap(ctx_near[0], 1)
 
-    def tail_of(part):
-        tail = part[rows + EDGE : rows + 3 * EDGE]
-        return jnp.concatenate([tail[:EDGE], tail[EDGE:]], axis=1)
-
-    member = lax.axis_index("seq") % GROUP
-    near_tail, diagonal, beyond = tail_of(kv_group[1]), tail_of(kv_group[3]), tail_of(kv_halo[3])
-    other_tail = jnp.where((member == 0) | (member == GROUP - 1), beyond, diagonal)
-    odd = member % 2 == 1
-    before = jnp.where(odd, near_tail, other_tail)
-    after = jnp.where(odd, other_tail, near_tail)
-
-    around = (residual, before, after, depth_kernel)
+    near_tail = kv_group[1][rows + EDGE : rows + 3 * EDGE]
+    around = (residual, near_tail, ctx_3, depth_kernel)
     early = (0, 2, 3)
     mixed, conv = convolve_early(early, lengths, [ctx_near[1], ctx_2, ctx_3], *around)
     late = (1,)

time: 60.3 us -> 60 us (level)
  the two profiles are of different devices: /device:TPU:16 before, /device:TPU:0 now
where the time goes in v4:
time: 60 us; the launch traced here: 60.1 us
  Pallas kernels  25 us (42%)
  starting transfers between devices  21.1 us (35%)
  waiting for transfers between devices  13.7 us (23%)
    pallas_call x2, Pallas kernels, attend(): pl.pallas_call(functools.partial(attend_kernel, rows, q_rows, widths, ms,...  15.6 us
    ppermute x9, starting transfers between devices, swap(): return lax.ppermute(array, 'seq', [(i, i ^ m) for i in range(peers)])  15 us
    ppermute x9, waiting for transfers between devices, swap(): return lax.ppermute(array, 'seq', [(i, i ^ m) for i in range(peers)])  13.7 us
    ppermute x3, starting transfers between devices, move(): lax.ppermute(array, 'seq', [(i, j) for i, j in pairs if 0 <= j < peers])  6.08 us
    pallas_call x1, Pallas kernels, finish(): pl.pallas_call(functools.partial(finish_kernel, BLOCK_ROWS, ms, early), o...  3.51 us
    pallas_call x1, Pallas kernels, convolve_early(): pl.pallas_call(functools.partial(convolve_kernel, BLOCK_ROWS, ms), out_sh...  3.31 us
    pallas_call x1, Pallas kernels, split_columns(): pl.pallas_call(functools.partial(split_kernel, cols), out_shape=[jax.Shap...  2.62 us
  transfers between devices with their start and end apart: 12, of which 4 were waited for; matrix products, arithmetic and copies ran while one was open for 0% of the time, Pallas kernels for 31%

profile of v4, /device:TPU:0, one launch (start us, length us, event | category | flops | bytes accessed | tf_op | source)
XLA Modules:
  0.0 60.1 jit_solution(44363832033369478)
XLA Ops:
  0.0 2.6 %split_columns.1 = (bf16[368,512]{1,0:T(8,128)(2,1)}, bf16[368,512]{1,0:T(8,128)(2,1)}, bf16[336,512]{1,0:T(8,128)(2,1)}, bf16[336,512]{1,0:T(8,128)(2,1)}, bf16...) custom-call(bf16[320,1024]{1,0:T(8,128)(2,1)} %query.1, ...), custom_call_target="tpu_custom_call" | custom-call | tf_op jit(solution)/shard_map/split_columns/pallas_call | solution.py:106
  2.6 0.0 copy-start.4
  2.7 3.0 %collective-permute-start = (bf16[368,512]{1,0:T(8,128)(2,1)}, bf16[368,512]{1,0:T(8,128)(2,1)S(1)}, u32[]{:S(2)}, u32[]{:S(2)}) collective-permute-start(bf16[368,512]{1,0:T(8,128)(2,1)} %get-tuple-element.27), channel_id=1, source_target_pairs={{0,2},{2,0},{4,6},{6,4},{8,10},{10,8},{12,14},{14,12},{16,18},{18,... | collective-permute-start | bytes 1130504 | tf_op jit(solution)/shard_map/ppermute | solution.py:486
  5.7 1.5 %collective-permute-start.2 = (bf16[336,512]{1,0:T(8,128)(2,1)}, bf16[336,512]{1,0:T(8,128)(2,1)S(1)}, u32[]{:S(2)}, u32[]{:S(2)}) collective-permute-start(bf16[336,512]{1,0:T(8,128)(2,1)} %get-tuple-element.31), channel_id=1, source_target_pairs={{0,6},{2,4},{4,2},{6,0},{8,14},{10,12},{12,10},{14,8},{16,22},{18,... | collective-permute-start | bytes 1032200 | tf_op jit(solution)/shard_map/ppermute | solution.py:486
  7.2 0.0 collective-permute-start.1
  7.2 1.3 %collective-permute-start.6 = (bf16[368,512]{1,0:T(8,128)(2,1)}, bf16[368,512]{1,0:T(8,128)(2,1)S(1)}, u32[]{:S(2)}, u32[]{:S(2)}) collective-permute-start(bf16[368,512]{1,0:T(8,128)(2,1)} %get-tuple-element.24.refs_0_), channel_id=1, source_target_pairs={{4,12},{6,14},{8,0},{10,2},{12,20},{14,22},{16,8},{18,10},{20,28},... | collective-permute-start | bytes 1130504 | tf_op jit(solution)/shard_map/ppermute | solution.py:490
  8.5 7.0 %collective-permute-done.refs_1_ = bf16[368,512]{1,0:T(8,128)(2,1)S(1)} collective-permute-done((bf16[368,512]{1,0:T(8,128)(2,1)}, bf16[368,512]{1,0:T(8,128)(2,1)S(1)}, u32[]{:S(2)}, u32[]{:S(2)}) %collective-permute-start) | collective-permute-done | bytes 376864 | tf_op jit(solution)/shard_map/ppermute | solution.py:486
  15.5 1.3 %collective-permute-start.7 = (bf16[368,512]{1,0:T(8,128)(2,1)S(1)}, bf16[368,512]{1,0:T(8,128)(2,1)S(1)}, u32[]{:S(2)}, u32[]{:S(2)}) collective-permute-start(bf16[368,512]{1,0:T(8,128)(2,1)S(1)} %collective-permute-done.refs_1_), channel_id=1, source_target_pairs={{4,12},{6,14},{8,0},{10,2},{12,20},{14,22},{16,8},{18,10},{20,28},... | collective-permute-start | bytes 1130504 | tf_op jit(solution)/shard_map/ppermute | solution.py:490
  16.8 5.3 %collective-permute-start.8 = (bf16[320,256]{1,0:T(8,128)(2,1)}, bf16[320,256]{1,0:T(8,128)(2,1)S(1)}, u32[]{:S(2)}, u32[]{:S(2)}) collective-permute-start(bf16[320,256]{1,0:T(8,128)(2,1)} %get-tuple-element.36), channel_id=1, source_target_pairs={{0,6},{2,4},{4,2},{6,0},{8,14},{10,12},{12,10},{14,8},{16,22},{18,... | collective-permute-start | bytes 491528 | tf_op jit(solution)/shard_map/ppermute | solution.py:486
  22.1 2.4 %collective-permute-done.2.refs_3_ = bf16[336,512]{1,0:T(8,128)(2,1)S(1)} collective-permute-done((bf16[336,512]{1,0:T(8,128)(2,1)}, bf16[336,512]{1,0:T(8,128)(2,1)S(1)}, u32[]{:S(2)}, u32[]{:S(2)}) %collective-permute-start.2) | collective-permute-done | bytes 344096 | tf_op jit(solution)/shard_map/ppermute | solution.py:486
  24.5 3.6 %collective-permute-done.1.refs_2_ = bf16[336,512]{1,0:T(8,128)(2,1)S(1)} collective-permute-done((bf16[336,512]{1,0:T(8,128)(2,1)}, bf16[336,512]{1,0:T(8,128)(2,1)S(1)}, u32[]{:S(2)}, u32[]{:S(2)}) %collective-permute-start.1) | collective-permute-done | bytes 344096 | tf_op jit(solution)/shard_map/ppermute | solution.py:486
  28.1 3.5 %collective-permute-start.3 = (bf16[672,512]{1,0:T(8,128)(2,1)S(1)}, bf16[672,512]{1,0:T(8,128)(2,1)S(1)}, u32[]{:S(2)}, u32[]{:S(2)}) collective-permute-start(bf16[672,512]{1,0:T(8,128)(2,1)S(1)} %pad_maximum_fusion), channel_id=1, source_target_pairs={{0,8},{2,10},{8,16},{10,18},{12,4},{14,6},{16,24},{18,26},{20,12},... | collective-permute-start | bytes 2064392 | tf_op jit(solution)/shard_map/ppermute | solution.py:490
  31.7 1.6 %collective-permute-start.4 = (bf16[320,256]{1,0:T(8,128)(2,1)S(1)}, bf16[320,256]{1,0:T(8,128)(2,1)S(1)}, u32[]{:S(2)}, u32[]{:S(2)}) collective-permute-start(bf16[320,256]{1,0:T(8,128)(2,1)S(1)} %copy-done.7), channel_id=1, source_target_pairs={{0,2},{2,0},{4,6},{6,4},{8,10},{10,8},{12,14},{14,12},{16,18},{18,... | collective-permute-start | bytes 491528 | tf_op jit(solution)/shard_map/ppermute | solution.py:486
  33.3 8.0 %attend.3 = (bf16[416,256]{1,0:T(8,128)(2,1)S(1)}, bf16[352,256]{1,0:T(8,128)(2,1)S(1)}) custom-call(s32[16]{0:T(128)S(1)} %copy-done.4, bf16[368,512]{1,0:T(8,128)(2,1)S(1)} %copy-done.5, bf16[368,512]{1,0:T(8,128)(2,1)S(1)} %collective-permute-done.refs_1_, bf16[336,512]{1,0:T(8,128)(2,1)S(1)} %collective-permute-done.1.refs_2_, ...), custom_call_target="tpu_custom_call" | custom-call | flops 11072962560 | bytes 3932160 | tf_op jit(solution)/shard_map/attend/pallas_call | solution.py:297
  41.3 0.1 collective-permute-start.10
  41.4 2.0 %collective-permute-start.11 = (bf16[352,256]{1,0:T(8,128)(2,1)S(1)}, bf16[352,256]{1,0:T(8,128)(2,1)S(1)}, u32[]{:S(2)}, u32[]{:S(2)}) collective-permute-start(bf16[352,256]{1,0:T(8,128)(2,1)S(1)} %get-tuple-element.40), channel_id=1, source_target_pairs={{0,4},{2,6},{4,0},{6,2},{8,12},{10,14},{12,8},{14,10},{16,20},{18,... | collective-permute-start | bytes 540680 | tf_op jit(solution)/shard_map/ppermute | solution.py:486
  43.4 0.0 copy-start
  43.4 0.0 copy-start.1
  43.5 7.6 %attend.2 = (bf16[352,256]{1,0:T(8,128)(2,1)S(1)}, bf16[352,256]{1,0:T(8,128)(2,1)S(1)}) custom-call(s32[16]{0:T(128)S(1)} %copy-done.4, bf16[368,512]{1,0:T(8,128)(2,1)S(1)} %copy-done.5, bf16[368,512]{1,0:T(8,128)(2,1)S(1)} %collective-permute-done.refs_1_, bf16[336,512]{1,0:T(8,128)(2,1)S(1)} %collective-permute-done.1.refs_2_, ...), custom_call_target="tpu_custom_call" | custom-call | flops 11072962560 | bytes 3932160 | tf_op jit(solution)/shard_map/attend/pallas_call | solution.py:297
  51.0 1.6 %collective-permute-start.5 = (bf16[352,256]{1,0:T(8,128)(2,1)S(1)}, bf16[352,256]{1,0:T(8,128)(2,1)S(1)}, u32[]{:S(2)}, u32[]{:S(2)}) collective-permute-start(bf16[352,256]{1,0:T(8,128)(2,1)S(1)} %get-tuple-element.35), channel_id=1, source_target_pairs={{0,2},{2,0},{4,6},{6,4},{8,10},{10,8},{12,14},{14,12},{16,18},{18,... | collective-permute-start | bytes 540680 | tf_op jit(solution)/shard_map/ppermute | solution.py:486
  52.6 0.0 copy-start.2
  52.7 3.3 %convolve.1 = (bf16[6,320,128]{2,1,0:T(8,128)(2,1)S(1)}, f32[6,320,128]{2,1,0:T(8,128)S(1)}) custom-call(s32[16]{0:T(128)S(1)} %copy-done.4, bf16[352,256]{1,0:T(8,128)(2,1)S(1)} %get-tuple-element.39.refs_0_, bf16[352,256]{1,0:T(8,128)(2,1)S(1)} %collective-permute-done.11.refs_1_, bf16[416,256]{1,0:T(8,128)(2,1)S(1)} %collective-permute-done.10.refs_2_.refs_5_.refs_3_, ...), custom_call_target="tpu_custom_call" | custom-call | flops 761856000 | bytes 2621440 | tf_op jit(solution)/shard_map/convolve/pallas_call | solution.py:445
  56.0 0.6 %collective-permute-done.5.refs_0_ = bf16[352,256]{1,0:T(8,128)(2,1)S(1)} collective-permute-done((bf16[352,256]{1,0:T(8,128)(2,1)S(1)}, bf16[352,256]{1,0:T(8,128)(2,1)S(1)}, u32[]{:S(2)}, u32[]{:S(2)}) %collective-permute-start.5) | collective-permute-done | bytes 180256 | tf_op jit(solution)/shard_map/ppermute | solution.py:486
  56.6 3.5 %finish.1 = bf16[320,1024]{1,0:T(8,128)(2,1)} custom-call(s32[16]{0:T(128)S(1)} %copy-done.4, bf16[352,256]{1,0:T(8,128)(2,1)S(1)} %collective-permute-done.5.refs_0_, bf16[320,1024]{1,0:T(8,128)(2,1)S(1)} %copy-done, bf16[32,512]{1,0:T(8,128)(2,1)S(1)} %slice.11.refs_4_.refs_2_, bf16[416,256]{1,0:T(8,128)(2,1)S(1)} %collective-permute-done.10.refs_2_.refs_5_.refs_3_, ...), custom_call_target="tpu_custom_call" | custom-call | tf_op jit(solution)/shard_map/finish/pallas_call | solution.py:465
  (24 shorter events, 0.1 us)
Async XLA Ops:
  2.6 29.1 %copy-start.7 = (bf16[320,256]{1,0:T(8,128)(2,1)S(1)}, bf16[320,256]{1,0:T(8,128)(2,1)}, u32[]{:S(2)}) copy-start(bf16[320,256]{1,0:T(8,128)(2,1)} %get-tuple-element.33) | copy-start | bytes 491524
  2.6 30.6 %copy-start.4 = (s32[16]{0:T(128)S(1)}, s32[16]{0:T(128)}, u32[]{:S(2)}) copy-start(s32[16]{0:T(128)} %lengths.7) | copy-start | bytes 196
  2.7 30.6 %copy-start.5 = (bf16[368,512]{1,0:T(8,128)(2,1)S(1)}, bf16[368,512]{1,0:T(8,128)(2,1)}, u32[]{:S(2)}) copy-start(bf16[368,512]{1,0:T(8,128)(2,1)} %get-tuple-element.24.refs_0_) | copy-start | bytes 1130500
  2.7 12.8 %collective-permute-start = (bf16[368,512]{1,0:T(8,128)(2,1)}, bf16[368,512]{1,0:T(8,128)(2,1)S(1)}, u32[]{:S(2)}, u32[]{:S(2)}) collective-permute-start(bf16[368,512]{1,0:T(8,128)(2,1)} %get-tuple-element.27), channel_id=1, source_target_pairs={{0,2},{2,0},{4,6},{6,4},{8,10},{10,8},{12,14},{14,12},{16,18},{18,... | collective-permute-start | bytes 1130504 | tf_op jit(solution)/shard_map/ppermute | solution.py:486
  5.7 18.8 %collective-permute-start.2 = (bf16[336,512]{1,0:T(8,128)(2,1)}, bf16[336,512]{1,0:T(8,128)(2,1)S(1)}, u32[]{:S(2)}, u32[]{:S(2)}) collective-permute-start(bf16[336,512]{1,0:T(8,128)(2,1)} %get-tuple-element.31), channel_id=1, source_target_pairs={{0,6},{2,4},{4,2},{6,0},{8,14},{10,12},{12,10},{14,8},{16,22},{18,... | collective-permute-start | bytes 1032200 | tf_op jit(solution)/shard_map/ppermute | solution.py:486
  7.2 20.9 %collective-permute-start.1 = (bf16[336,512]{1,0:T(8,128)(2,1)}, bf16[336,512]{1,0:T(8,128)(2,1)S(1)}, u32[]{:S(2)}, u32[]{:S(2)}) collective-permute-start(bf16[336,512]{1,0:T(8,128)(2,1)} %get-tuple-element.29), channel_id=1, source_target_pairs={{0,4},{2,6},{4,0},{6,2},{8,12},{10,14},{12,8},{14,10},{16,20},{18,... | collective-permute-start | bytes 1032200 | tf_op jit(solution)/shard_map/ppermute | solution.py:486
  7.2 24.5 %collective-permute-start.6 = (bf16[368,512]{1,0:T(8,128)(2,1)}, bf16[368,512]{1,0:T(8,128)(2,1)S(1)}, u32[]{:S(2)}, u32[]{:S(2)}) collective-permute-start(bf16[368,512]{1,0:T(8,128)(2,1)} %get-tuple-element.24.refs_0_), channel_id=1, source_target_pairs={{4,12},{6,14},{8,0},{10,2},{12,20},{14,22},{16,8},{18,10},{20,28},... | collective-permute-start | bytes 1130504 | tf_op jit(solution)/shard_map/ppermute | solution.py:490
  15.5 17.8 %collective-permute-start.7 = (bf16[368,512]{1,0:T(8,128)(2,1)S(1)}, bf16[368,512]{1,0:T(8,128)(2,1)S(1)}, u32[]{:S(2)}, u32[]{:S(2)}) collective-permute-start(bf16[368,512]{1,0:T(8,128)(2,1)S(1)} %collective-permute-done.refs_1_), channel_id=1, source_target_pairs={{4,12},{6,14},{8,0},{10,2},{12,20},{14,22},{16,8},{18,10},{20,28},... | collective-permute-start | bytes 1130504 | tf_op jit(solution)/shard_map/ppermute | solution.py:490
  16.8 16.5 %collective-permute-start.8 = (bf16[320,256]{1,0:T(8,128)(2,1)}, bf16[320,256]{1,0:T(8,128)(2,1)S(1)}, u32[]{:S(2)}, u32[]{:S(2)}) collective-permute-start(bf16[320,256]{1,0:T(8,128)(2,1)} %get-tuple-element.36), channel_id=1, source_target_pairs={{0,6},{2,4},{4,2},{6,0},{8,14},{10,12},{12,10},{14,8},{16,22},{18,... | collective-permute-start | bytes 491528 | tf_op jit(solution)/shard_map/ppermute | solution.py:486
  24.5 8.8 %collective-permute-start.9 = (bf16[320,256]{1,0:T(8,128)(2,1)}, bf16[320,256]{1,0:T(8,128)(2,1)S(1)}, u32[]{:S(2)}, u32[]{:S(2)}) collective-permute-start(bf16[320,256]{1,0:T(8,128)(2,1)} %get-tuple-element.37), channel_id=1, source_target_pairs={{0,4},{2,6},{4,0},{6,2},{8,12},{10,14},{12,8},{14,10},{16,20},{18,... | collective-permute-start | bytes 491528 | tf_op jit(solution)/shard_map/ppermute | solution.py:486
  28.1 15.2 %collective-permute-start.3 = (bf16[672,512]{1,0:T(8,128)(2,1)S(1)}, bf16[672,512]{1,0:T(8,128)(2,1)S(1)}, u32[]{:S(2)}, u32[]{:S(2)}) collective-permute-start(bf16[672,512]{1,0:T(8,128)(2,1)S(1)} %pad_maximum_fusion), channel_id=1, source_target_pairs={{0,8},{2,10},{8,16},{10,18},{12,4},{14,6},{16,24},{18,26},{20,12},... | collective-permute-start | bytes 2064392 | tf_op jit(solution)/shard_map/ppermute | solution.py:490
  31.7 11.7 %collective-permute-start.4 = (bf16[320,256]{1,0:T(8,128)(2,1)S(1)}, bf16[320,256]{1,0:T(8,128)(2,1)S(1)}, u32[]{:S(2)}, u32[]{:S(2)}) collective-permute-start(bf16[320,256]{1,0:T(8,128)(2,1)S(1)} %copy-done.7), channel_id=1, source_target_pairs={{0,2},{2,0},{4,6},{6,4},{8,10},{10,8},{12,14},{14,12},{16,18},{18,... | collective-permute-start | bytes 491528 | tf_op jit(solution)/shard_map/ppermute | solution.py:486
  41.3 2.1 %copy-start.6 = (bf16[320,256]{1,0:T(8,128)(2,1)S(1)}, bf16[320,256]{1,0:T(8,128)(2,1)}, u32[]{:S(2)}) copy-start(bf16[320,256]{1,0:T(8,128)(2,1)} %get-tuple-element.34.refs_7_) | copy-start | bytes 491524
  41.3 11.3 %collective-permute-start.10 = (bf16[416,256]{1,0:T(8,128)(2,1)S(1)}, bf16[416,256]{1,0:T(8,128)(2,1)S(1)}, u32[]{:S(2)}, u32[]{:S(2)}) collective-permute-start(bf16[416,256]{1,0:T(8,128)(2,1)S(1)} %get-tuple-element.38), channel_id=1, source_target_pairs={{0,6},{2,4},{4,2},{6,0},{8,14},{10,12},{12,10},{14,8},{16,22},{18,... | collective-permute-start | bytes 638984 | tf_op jit(solution)/shard_map/ppermute | solution.py:486
  41.4 11.2 %collective-permute-start.11 = (bf16[352,256]{1,0:T(8,128)(2,1)S(1)}, bf16[352,256]{1,0:T(8,128)(2,1)S(1)}, u32[]{:S(2)}, u32[]{:S(2)}) collective-permute-start(bf16[352,256]{1,0:T(8,128)(2,1)S(1)} %get-tuple-element.40), channel_id=1, source_target_pairs={{0,4},{2,6},{4,0},{6,2},{8,12},{10,14},{12,8},{14,10},{16,20},{18,... | collective-permute-start | bytes 540680 | tf_op jit(solution)/shard_map/ppermute | solution.py:486
  43.4 9.2 %copy-start = (bf16[320,1024]{1,0:T(8,128)(2,1)S(1)}, bf16[320,1024]{1,0:T(8,128)(2,1)}, u32[]{:S(2)}) copy-start(bf16[320,1024]{1,0:T(8,128)(2,1)} %refs_1_.1) | copy-start | bytes 1966084
  43.4 9.2 %copy-start.1 = (f32[31,1024]{1,0:T(8,128)S(1)}, f32[31,1024]{1,0:T(8,128)}, u32[]{:S(2)}) copy-start(f32[31,1024]{1,0:T(8,128)} %refs_4_.1) | copy-start | bytes 380932
  51.0 5.6 %collective-permute-start.5 = (bf16[352,256]{1,0:T(8,128)(2,1)S(1)}, bf16[352,256]{1,0:T(8,128)(2,1)S(1)}, u32[]{:S(2)}, u32[]{:S(2)}) collective-permute-start(bf16[352,256]{1,0:T(8,128)(2,1)S(1)} %get-tuple-element.35), channel_id=1, source_target_pairs={{0,2},{2,0},{4,6},{6,4},{8,10},{10,8},{12,14},{14,12},{16,18},{18,... | collective-permute-start | bytes 540680 | tf_op jit(solution)/shard_map/ppermute | solution.py:486
  52.6 4.0 %copy-start.2 = (f32[1024]{0:T(1024)S(1)}, f32[1024]{0:T(1024)}, u32[]{:S(2)}) copy-start(f32[1024]{0:T(1024)} %param.14) | copy-start | bytes 12292
  52.7 4.0 %copy-start.3 = (f32[1024]{0:T(1024)S(1)}, f32[1024]{0:T(1024)}, u32[]{:S(2)}) copy-start(f32[1024]{0:T(1024)} %param.15) | copy-start | bytes 12292
